TPU v7x, 32 devices: a whole 2x2x4 slice. The times are simulated.
32 devices in a mesh: section: 2 (over y), grp: 4 (over x, core), tok: 4 (over z).
Axes of the slice: x: 2, y: 2, z: 4, core: 2. Of those that a mesh axis runs over, the one named last changes fastest.
Arguments:
- image_in: bfloat16 [2, 4, 128, 3072], P('section', 'grp', 'tok'), may hold values from -1.5 to 1.5
- text_in: bfloat16 [2, 4, 512, 3072], P('section', 'grp', 'tok'), may hold values from -1.5 to 1.5
- text_length: int32 [4], P('grp'), may hold values from 256 to 512, as said below
- entry_order: int32 [4, 4], P('grp'), may hold values from 0 to 3, as said below
- step_index: int32 [4, 4], P('grp'), may hold values from 0 to 3
- image_modulation: bfloat16 [2, 4, 18432], P('section'), may hold values from -3 to 3
- text_modulation: bfloat16 [2, 4, 9216], P('section'), may hold values from -3 to 3
- image_to_heads: bfloat16 [2, 3072, 9216], P('section', None, 'tok'), may hold values from -0.109375 to 0.109375
- text_to_heads: bfloat16 [2, 3072, 9216], P('section', None, 'tok'), may hold values from -0.109375 to 0.109375
- head_gain: float32 [2, 4, 128], P('section'), may hold values from 0.5 to 2
- image_from_heads: bfloat16 [2, 3072, 3072], P('section', None, 'tok'), may hold values from -0.109375 to 0.109375
- text_from_heads: bfloat16 [2, 3072, 3072], P('section', None, 'tok'), may hold values from -0.109375 to 0.109375
- image_up: bfloat16 [2, 3072, 12288], P('section', None, 'tok'), may hold values from -0.109375 to 0.109375
- image_down: bfloat16 [2, 12288, 3072], P('section', 'tok'), may hold values from -0.0546875 to 0.0546875
- stale_cache: bfloat16 [2, 4, 512, 6144], P('section', 'grp', 'tok'), may hold values from -400 to 400
- final_modulation: bfloat16 [4, 6144], replicated, may hold values from -3 to 3
- final_weight: bfloat16 [3072, 64], P(None, 'section'), may hold values from -0.109375 to 0.109375
- latents: float32 [4, 128, 64], P('grp', 'tok', 'section'), may hold values from -6 to 6
Outputs:
- image_handoff: bfloat16 [2, 4, 128, 3072], P('section', 'grp', 'tok')
- text_handoff: bfloat16 [2, 4, 512, 3072], P('section', 'grp', 'tok')
- fresh_cache: bfloat16 [2, 4, 512, 6144], P('section', 'grp', 'tok')
- latents_next: float32 [4, 128, 64], P('grp', 'tok', 'section')
Inputs may be any that keep to these rules, and one draw needn't show every extreme that they name: `text_length`: valid text tokens of each request; some request has exactly 512. `entry_order`: each row is a permutation of the 4 patch numbers.
All inputs are finite; a program needn't handle non-finite values.
Results may differ from a plain program's by a relative error of at most 0.023.
The roundings to bfloat16 on the way count: a program that leaves them out, or rounds other values in their place, can miss the bound.
Values may be sent and summed in bfloat16 or wider, within the bound.
A program may use at most 192 MiB of HBM per device.

v0:
```python
import jax
import jax.numpy as jnp
from jax import lax
from jax.sharding import PartitionSpec as P

HDIM = 128
TSTEPS = 4


eps = 1e-06
masked_score = -1e30


def from_behind(block, axis, distance):
    devices = range(lax.axis_size(axis))
    route = [((i - distance) % len(devices), i) for i in devices]
    return lax.ppermute(block, axis, route)


def layer_norm(field):
    mean = jnp.mean(field, axis=-1, keepdims=True)
    centred = field - mean
    spread = jnp.mean(centred * centred, axis=-1, keepdims=True)
    return centred * lax.rsqrt(spread + eps)


def modulate(field, shift, scale):
    return layer_norm(field) * (1.0 + scale) + shift


def head_norm(field, gain):
    height, width = field.shape
    shaped = field.reshape(height, width // HDIM, HDIM)
    power = jnp.mean(shaped * shaped, axis=-1, keepdims=True)
    return (shaped * lax.rsqrt(power + eps) * gain).reshape(height, width)


def attend(carry, queries, piece, valid):
    highest, total, mixed = carry
    height, width = queries.shape
    heads = width // HDIM
    keys = piece[:, :width].reshape(-1, heads, HDIM)
    values = piece[:, width:].reshape(-1, heads, HDIM)
    scores = jnp.einsum(
        "qhd,khd->qhk",
        queries.reshape(height, heads, HDIM),
        keys,
        preferred_element_type=jnp.float32,
    ) * HDIM ** (-0.5)
    scores = jnp.where(valid[None, None, :], scores, masked_score)
    new_high = jnp.maximum(highest, jnp.max(scores, axis=-1))
    expo = jnp.where(valid[None, None, :], jnp.exp(scores - new_high[..., None]), 0.0)
    keep = jnp.exp(highest - new_high)
    total = total * keep + jnp.sum(expo, axis=-1)
    mixed = mixed * keep[..., None] + jnp.einsum(
        "qhk,khd->qhd", expo.astype(jnp.bfloat16), values, preferred_element_type=jnp.float32
    )
    return (new_high, total, mixed)


def empty_carry(height, heads):
    return (
        jnp.full((height, heads), masked_score, jnp.float32),
        jnp.zeros((height, heads), jnp.float32),
        jnp.zeros((height, heads, HDIM), jnp.float32),
    )


def shards(
    image_in,
    text_in,
    text_length,
    entry_order,
    step_index,
    image_modulation,
    text_modulation,
    image_to_heads,
    text_to_heads,
    head_gain,
    image_from_heads,
    text_from_heads,
    image_up,
    image_down,
    stale_cache,
    final_modulation,
    final_weight,
    latents,
):
    section = lax.axis_index("section")
    last_section = lax.axis_size("section") - 1
    position = lax.axis_index("tok")
    image_x = image_in[0, 0].astype(jnp.float32)
    text_x = text_in[0, 0].astype(jnp.float32)
    image_rows = image_x.shape[0]
    width = image_x.shape[1]
    heads = width // HDIM
    patch = lax.dynamic_index_in_dim(entry_order[0], section, 0, False)
    step_now = lax.dynamic_index_in_dim(step_index[0], patch, 0, False)
    modul = (
        lax.dynamic_index_in_dim(image_modulation[0], step_now, 0, False)
        .astype(jnp.float32)
        .reshape(6, width)
    )
    text_mod = (
        lax.dynamic_index_in_dim(text_modulation[0], step_now, 0, False)
        .astype(jnp.float32)
        .reshape(3, width)
    )
    image_normed = modulate(image_x, modul[0], modul[1]).astype(jnp.bfloat16)
    text_normed = modulate(text_x, text_mod[0], text_mod[1]).astype(jnp.bfloat16)
    every_image, every_text = (
        lax.all_gather(image_normed, "tok", axis=0, tiled=True),
        lax.all_gather(text_normed, "tok", axis=0, tiled=True),
    )
    image_cols = jnp.dot(every_image, image_to_heads[0], preferred_element_type=jnp.float32).astype(
        jnp.bfloat16
    )
    text_cols = jnp.dot(every_text, text_to_heads[0], preferred_element_type=jnp.float32).astype(
        jnp.bfloat16
    )
    image_proj, text_proj = (
        lax.all_to_all(image_cols, "tok", split_axis=0, concat_axis=1, tiled=True),
        lax.all_to_all(text_cols, "tok", split_axis=0, concat_axis=1, tiled=True),
    )
    gains = head_gain[0]
    image_query = head_norm(image_proj[:, :width].astype(jnp.float32), gains[0]).astype(
        jnp.bfloat16
    )
    image_key = head_norm(image_proj[:, width : 2 * width].astype(jnp.float32), gains[1]).astype(
        jnp.bfloat16
    )
    text_query = head_norm(text_proj[:, :width].astype(jnp.float32), gains[2]).astype(jnp.bfloat16)
    text_key = head_norm(text_proj[:, width : 2 * width].astype(jnp.float32), gains[3]).astype(
        jnp.bfloat16
    )
    fresh_image = jnp.concatenate([image_key, image_proj[:, 2 * width :]], axis=1)
    fresh_text = jnp.concatenate([text_key, text_proj[:, 2 * width :]], axis=1)
    queries = jnp.concatenate([image_query, text_query], axis=0)
    query_rows = queries.shape[0]
    patch_rows = lax.all_gather(fresh_image, "tok", axis=0, tiled=True)
    stale = stale_cache[0, 0]
    cache_rows = stale.shape[0]
    patch_len = patch_rows.shape[0]
    first_row = position * cache_rows
    begin = patch * patch_len
    offset = jnp.clip(first_row - begin, 0, patch_len - cache_rows)
    window = lax.dynamic_slice_in_dim(patch_rows, offset, cache_rows, 0)
    inside = jnp.logical_and(first_row >= begin, first_row < begin + patch_len)
    current = jnp.where(inside, window, stale)
    text_count = text_length[0]
    piece = lax.all_gather(current, "tok", axis=0, tiled=True)
    carry = attend(
        empty_carry(query_rows, heads), queries, piece, jnp.ones((piece.shape[0],), bool)
    )
    piece = lax.all_gather(fresh_text, "tok", axis=0, tiled=True)
    where_text = jnp.arange(piece.shape[0], dtype=jnp.int32)
    highest, total, mixed = attend(carry, queries, piece, where_text < text_count)
    attended = (mixed / total[..., None]).reshape(query_rows, width).astype(jnp.bfloat16)
    every_image_att, every_text_att = (
        lax.all_gather(attended[:image_rows], "tok", axis=0, tiled=True),
        lax.all_gather(attended[image_rows:], "tok", axis=0, tiled=True),
    )
    image_back_cols = jnp.dot(
        every_image_att, image_from_heads[0], preferred_element_type=jnp.float32
    ).astype(jnp.bfloat16)
    text_back_cols = jnp.dot(
        every_text_att, text_from_heads[0], preferred_element_type=jnp.float32
    ).astype(jnp.bfloat16)
    image_back, text_back = (
        lax.all_to_all(image_back_cols, "tok", split_axis=0, concat_axis=1, tiled=True),
        lax.all_to_all(text_back_cols, "tok", split_axis=0, concat_axis=1, tiled=True),
    )
    image_mid = image_x + modul[2] * image_back.astype(jnp.float32)
    text_out = (text_x + text_mod[2] * text_back.astype(jnp.float32)).astype(jnp.bfloat16)
    mlp_normed = modulate(image_mid, modul[3], modul[4]).astype(jnp.bfloat16)
    up_weight = image_up[0]
    down_weight = image_down[0]
    hidden = jax.nn.gelu(
        jnp.dot(
            lax.all_gather(mlp_normed, "tok", axis=0, tiled=True),
            up_weight,
            preferred_element_type=jnp.float32,
        ),
        approximate=True,
    ).astype(jnp.bfloat16)
    reduced = lax.psum_scatter(
        jnp.dot(hidden, down_weight, preferred_element_type=jnp.float32),
        "tok",
        scatter_dimension=0,
        tiled=True,
    )
    image_out = (image_mid + modul[5] * reduced).astype(jnp.bfloat16)
    joined = from_behind(jnp.concatenate([image_out, text_out], axis=0), "section", 1)
    image_next = joined[:image_rows]
    text_next = joined[image_rows:]
    final_source = jnp.where(section == last_section, image_out, image_next)
    patch_last = entry_order[0, last_section]
    step_last = lax.dynamic_index_in_dim(step_index[0], patch_last, 0, False)
    final_mod = (
        lax.dynamic_index_in_dim(final_modulation, step_last, 0, False)
        .astype(jnp.float32)
        .reshape(2, width)
    )
    normed = modulate(final_source.astype(jnp.float32), final_mod[0], final_mod[1]).astype(
        jnp.bfloat16
    )
    velocity = jnp.dot(normed, final_weight, preferred_element_type=jnp.float32)
    latents_next = latents[0] + -1.0 / TSTEPS * velocity
    return (image_next[None, None], text_next[None, None], current[None, None], latents_next[None])


def solution(mesh):
    placed = (
        P("section", "grp", "tok", None),
        P("section", "grp", "tok", None),
        P("grp"),
        P("grp", None),
        P("grp", None),
        P("section", None, None),
        P("section", None, None),
        P("section", None, "tok"),
        P("section", None, "tok"),
        P("section", None, None),
        P("section", None, "tok"),
        P("section", None, "tok"),
        P("section", None, "tok"),
        P("section", "tok", None),
        P("section", "grp", "tok", None),
        P(),
        P(None, "section"),
        P("grp", "tok", "section"),
    )
    return jax.shard_map(
        shards,
        mesh=mesh,
        in_specs=placed,
        out_specs=(
            P("section", "grp", "tok", None),
            P("section", "grp", "tok", None),
            P("section", "grp", "tok", None),
            P("grp", "tok", "section"),
        ),
        check_vma=False,
    )
```

profile of v0, /device:TPU:0, one launch (start us, length us, event | category | flops | bytes accessed | tf_op | source)
XLA Modules:
  0.0 659.3 jit_solution(13846519241160657208)
XLA Ops:
  7.2 1.3 fusion.121
  12.4 1.4 constant_dynamic-slice_fusion
  18.4 1.2 fusion.89
  20.6 21.3 %all_gather.24 = bf16[128,3072]{1,0:T(8,128)(2,1)S(1)} all-gather(bf16[32,3072]{1,0:T(8,128)(2,1)S(1)} %fusion.92), channel_id=1, replica_groups=mesh['section'=2,'grp'=4,'tok'=4] {'tok'}, dimensions={0}, use_global_device_ids=true | all-gather | bytes 983040 | tf_op jit(solution)/shard_map/all_gather | solution.py:112
  41.9 7.9 %fusion.34 = bf16[128,2304]{1,0:T(8,128)(2,1)} fusion(bf16[128,3072]{1,0:T(8,128)(2,1)S(1)} %all_gather.24, bf16[1,3072,2304]{2,1,0:T(8,128)(2,1)} %param.25), kind=kOutput, calls=%fused_computation.35 | convolution fusion | flops 1812234240 | bytes 15532032 | tf_op jit(solution)/shard_map/dot_general | solution.py:115
  49.9 3.5 all-to-all-start
  54.5 12.9 %all-to-all-done = bf16[4,32,2304]{2,1,0:T(8,128)(2,1)S(1)} async-done(((bf16[4,32,2304]{2,1,0:T(8,128)(2,1)}), bf16[4,32,2304]{2,1,0:T(8,128)(2,1)S(1)}, u32[]{:S(2)}, u32[]{:S(2)}) %all-to-all-start) | async-done | bytes 589856 | tf_op jit(solution)/shard_map/all_to_all | solution.py:122
  70.1 1.3 fusion.49
  71.5 1.9 copy.41
  74.0 31.7 %all-gather.6.cloned.1.call-done = bf16[128,6144]{1,0:T(8,128)(2,1)} async-done(((bf16[32,6144]{1,0:T(8,128)(2,1)}), bf16[128,6144]{1,0:T(8,128)(2,1)}) %all-gather.6.cloned.1.call-update) | async-done | bytes 1572880 | tf_op jit(solution)/shard_map/all_gather | solution.py:140
  105.8 2.6 copy.42
  108.3 1.3 bitcast_select_fusion
  109.7 60.6 %all-gather.10.cloned.1.call-done = bf16[512,3072]{1,0:T(8,128)(2,1)} async-done(((bf16[128,3072]{1,0:T(8,128)(2,1)}), bf16[512,3072]{1,0:T(8,128)(2,1)}) %all-gather.10.cloned.1.call-update) | async-done | bytes 3145744 | tf_op jit(solution)/shard_map/all_gather | solution.py:113
  170.3 12.4 %fusion.19 = bf16[512,2304]{1,0:T(8,128)(2,1)S(1)} fusion(bf16[512,3072]{1,0:T(8,128)(2,1)} %all-gather.10.cloned.1.call-done, bf16[1,3072,2304]{2,1,0:T(8,128)(2,1)} %param.26), kind=kOutput, calls=%fused_computation.24 | convolution fusion | flops 7248936960 | bytes 19660800 | tf_op jit(solution)/shard_map/dot_general | solution.py:118
  182.7 2.5 copy.43
  185.2 3.6 all-to-all-start.1
  188.9 1.2 broadcast_bitcast_fusion
  190.1 103.5 %all-to-all-done.1 = bf16[4,128,2304]{1,2,0:T(8,128)(2,1)S(1)} async-done(((bf16[4,128,2304]{1,2,0:T(8,128)(2,1)}), bf16[4,128,2304]{1,2,0:T(8,128)(2,1)S(1)}, u32[]{:S(2)}, u32[]{:S(2)}) %all-to-all-start.1) | async-done | bytes 2359328 | tf_op jit(solution)/shard_map/all_to_all | solution.py:123
  294.6 1.9 convert_multiply_fusion.3
  296.5 2.1 reduce_sum.133
  298.6 2.1 reduce_sum.132
  301.5 2.8 fusion.52
  304.3 1.2 pad_maximum_fusion
  306.9 29.7 %all-gather.8.cloned.1.call-done = bf16[512,6144]{0,1:T(8,128)(2,1)} async-done(((bf16[128,6144]{0,1:T(8,128)(2,1)}), bf16[512,6144]{0,1:T(8,128)(2,1)}) %all-gather.8.cloned.1.call-update) | async-done | bytes 6291472 | tf_op jit(solution)/shard_map/all_gather | solution.py:151
  336.6 4.9 fusion.117
  341.5 4.2 bitcast_reduce_fusion.1
  345.7 108.0 %all-gather.12.cloned.1.call-done = bf16[512,6144]{0,1:T(8,128)(2,1)} async-done(((bf16[128,6144]{0,1:T(8,128)(2,1)}), bf16[512,6144]{0,1:T(8,128)(2,1)}) %all-gather.12.cloned.1.call-update) | async-done | bytes 6291472 | tf_op jit(solution)/shard_map/all_gather | solution.py:155
  453.7 4.9 fusion.118
  458.6 1.5 bitcast_reduce_fusion
  460.1 2.5 fusion.13
  462.6 2.0 fusion.22
  464.8 1.1 slice-done.1
  465.9 2.2 fusion.11
  468.2 3.5 fusion.38
  471.8 1.2 copy.52
  473.0 24.8 %all_gather.29 = bf16[128,3072]{1,0:T(8,128)(2,1)S(1)} all-gather(bf16[32,3072]{1,0:T(8,128)(2,1)S(1)} %copy_bitcast_fusion), channel_id=1, replica_groups=mesh['section'=2,'grp'=4,'tok'=4] {'tok'}, dimensions={0}, use_global_device_ids=true | all-gather | bytes 983040 | tf_op jit(solution)/shard_map/all_gather | solution.py:160
  497.9 3.2 fusion.70
  501.1 21.3 %all_to_all.64 = bf16[4,32,768]{2,1,0:T(8,128)(2,1)S(1)} all-to-all(bf16[4,32,768]{2,1,0:T(8,128)(2,1)S(1)} %bitcast.252), channel_id=1, replica_groups=mesh['section'=2,'grp'=4,'tok'=4] {'tok'}, dimensions={0} | all-to-all | bytes 393216 | tf_op jit(solution)/shard_map/all_to_all | solution.py:170
  523.0 30.4 %all_gather.30 = bf16[128,3072]{1,0:T(8,128)(2,1)S(1)} all-gather(bf16[32,3072]{1,0:T(8,128)(2,1)S(1)} %add_convert_fusion.1), channel_id=1, replica_groups=mesh['section'=2,'grp'=4,'tok'=4] {'tok'}, dimensions={0}, use_global_device_ids=true | all-gather | bytes 983040 | tf_op jit(solution)/shard_map/all_gather | solution.py:180
  553.3 18.2 %fusion = f32[128,3072]{1,0:T(8,128)} fusion(bf16[1,3072,3072]{2,1,0:T(8,128)(2,1)} %param.31, bf16[128,3072]{1,0:T(8,128)(2,1)S(1)} %all_gather.30, bf16[1,3072,3072]{2,1,0:T(8,128)(2,1)} %param.30), kind=kOutput, calls=%fused_computation | convolution fusion | flops 4835377152 | bytes 40108032 | tf_op jit(solution)/shard_map/dot_general | solution.py:187
  571.7 6.8 %fusion.67 = bf16[512,768]{1,0:T(8,128)(2,1)} fusion(bf16[512,3072]{0,1:T(8,128)(2,1)} %all-gather.14.cloned.1.call-done, bf16[1,3072,768]{2,1,0:T(8,128)(2,1)} %param.29), kind=kOutput, calls=%fused_computation.72 | convolution fusion | flops 2416312320 | bytes 8650752 | tf_op jit(solution)/shard_map/dot_general | solution.py:166
  578.5 3.5 all-to-all-start.3
  583.9 35.7 %reduce-scatter.2.cloned.1.call-done = f32[32,3072]{1,0:T(8,128)} async-done(((f32[128,3072]{1,0:T(8,128)}), f32[32,3072]{1,0:T(8,128)}) %reduce-scatter.2.cloned.1.call-update) | async-done | bytes 393232 | tf_op jit(solution)/shard_map/reduce_scatter | solution.py:186
  622.8 1.6 collective-permute-start
  624.5 1.6 copy.54
  626.1 20.4 %collective-permute-done = bf16[160,3072]{1,0:T(8,128)(2,1)} collective-permute-done((bf16[160,3072]{1,0:T(8,128)(2,1)}, bf16[160,3072]{1,0:T(8,128)(2,1)}, u32[]{:S(2)}, u32[]{:S(2)}) %collective-permute-start) | collective-permute-done | bytes 983072 | tf_op jit(solution)/shard_map/ppermute | solution.py:17
  648.8 1.6 slice_bitcast_fusion.2
  650.4 2.1 slice_bitcast_fusion
  (105 shorter events, 16.5 us)
Async XLA Ops:
  7.2 640.7 %copy-start = (bf16[3072,32]{0,1:T(8,128)(2,1)S(1)}, bf16[3072,32]{0,1:T(8,128)(2,1)}, u32[]{:S(2)}) copy-start(bf16[3072,32]{0,1:T(8,128)(2,1)} %param.34) | copy-start | bytes 589828
  41.9 11.5 %copy-start.2 = (bf16[1,1,128,3072]{3,2,1,0:T(8,128)(2,1)S(1)}, bf16[1,1,128,3072]{3,2,1,0:T(8,128)(2,1)}, u32[]{:S(2)}) copy-start(bf16[1,1,128,3072]{3,2,1,0:T(8,128)(2,1)} %param.19) | copy-start | bytes 2359300
  41.9 12.1 %copy-start.14 = (f32[1,4,128]{2,1,0:T(4,128)S(1)}, f32[1,4,128]{2,1,0:T(4,128)}, u32[]{:S(2)}) copy-start(f32[1,4,128]{2,1,0:T(4,128)} %param.27) | copy-start | bytes 6148
  49.9 17.6 %all-to-all-start = ((bf16[4,32,2304]{2,1,0:T(8,128)(2,1)}), bf16[4,32,2304]{2,1,0:T(8,128)(2,1)S(1)}, u32[]{:S(2)}, u32[]{:S(2)}) async-start(bf16[4,32,2304]{2,1,0:T(8,128)(2,1)} %bitcast.7), calls=%async_computation | async-start | bytes 1179648 | tf_op jit(solution)/shard_map/all_to_all | solution.py:122
  53.3 52.4 %all-gather.6.cloned.1.call-start = ((), (), s32[]{:S(2)}) async-start(), calls=%async_computation.5 | async-start | bytes 1966080 | tf_op jit(solution)/shard_map/all_gather | solution.py:140
  67.5 1.9 copy-start.12
  69.4 100.9 %all-gather.10.cloned.1.call-start = ((), (), s32[]{:S(2)}) async-start(), calls=%async_computation.7 | async-start | bytes 3932160 | tf_op jit(solution)/shard_map/all_gather | solution.py:113
  71.4 265.2 %all-gather.8.cloned.1.call-start = ((), (), s32[]{:S(2)}) async-start(), calls=%async_computation.6 | async-start | bytes 7864320 | tf_op jit(solution)/shard_map/all_gather | solution.py:151
  185.2 108.5 %all-to-all-start.1 = ((bf16[4,128,2304]{1,2,0:T(8,128)(2,1)}), bf16[4,128,2304]{1,2,0:T(8,128)(2,1)S(1)}, u32[]{:S(2)}, u32[]{:S(2)}) async-start(bf16[4,128,2304]{1,2,0:T(8,128)(2,1)} %copy.43), calls=%async_computation.1 | async-start | bytes 4718592 | tf_op jit(solution)/shard_map/all_to_all | solution.py:123
  188.8 264.8 %all-gather.12.cloned.1.call-start = ((), (), s32[]{:S(2)}) async-start(), calls=%async_computation.8 | async-start | bytes 7864320 | tf_op jit(solution)/shard_map/all_gather | solution.py:155
  300.7 3.7 copy-start.5
  304.3 2.2 copy-start.4
  305.6 266.1 %all-gather.14.cloned.1.call-start = ((), (), s32[]{:S(2)}) async-start(), calls=%async_computation.10 | async-start | bytes 3932160 | tf_op jit(solution)/shard_map/all_gather | solution.py:161
  460.1 2.5 copy-start.7
  462.6 2.2 slice-start
  462.6 3.3 slice-start.1
  465.9 2.3 copy-start.6
  473.0 146.6 %reduce-scatter.2.cloned.1.call-start = ((), (), s32[]{:S(2)}) async-start(), calls=%async_computation.9 | async-start | bytes 1966080 | tf_op jit(solution)/shard_map/reduce_scatter | solution.py:186
  497.9 24.5 %copy-start.3 = (bf16[1,1,32,3072]{3,2,1,0:T(8,128)(2,1)S(1)}, bf16[1,1,32,3072]{3,2,1,0:T(8,128)(2,1)}, u32[]{:S(2)}) copy-start(bf16[1,1,32,3072]{3,2,1,0:T(8,128)(2,1)} %param.18) | copy-start | bytes 589828
  497.9 25.0 %copy-start.10 = (f32[1,1,3072]{2,1,0:T(1,128)S(1)}, f32[1,1,3072]{2,1,0:T(1,128)}, u32[]{:S(2)}) copy-start(f32[1,1,3072]{2,1,0:T(1,128)} %get-tuple-element.29) | copy-start | bytes 36868
  497.9 25.0 %copy-start.11 = (f32[1,1,3072]{2,1,0:T(1,128)S(1)}, f32[1,1,3072]{2,1,0:T(1,128)}, u32[]{:S(2)}) copy-start(f32[1,1,3072]{2,1,0:T(1,128)} %get-tuple-element.30) | copy-start | bytes 36868
  571.6 47.9 %copy-start.8 = (f32[1,1,3072]{2,1,0:T(1,128)S(1)}, f32[1,1,3072]{2,1,0:T(1,128)}, u32[]{:S(2)}) copy-start(f32[1,1,3072]{2,1,0:T(1,128)} %get-tuple-element.28) | copy-start | bytes 36868
  578.5 42.7 %all-to-all-start.3 = ((bf16[4,128,768]{2,1,0:T(8,128)(2,1)}), bf16[4,128,768]{2,1,0:T(8,128)(2,1)S(1)}, u32[]{:S(2)}, u32[]{:S(2)}) async-start(bf16[4,128,768]{2,1,0:T(8,128)(2,1)} %bitcast.51), calls=%async_computation.4 | async-start | bytes 1572864 | tf_op jit(solution)/shard_map/all_to_all | solution.py:171
  619.6 2.0 copy-start.9
  621.5 3.0 copy-start.13
  621.5 3.0 copy-start.1
  621.8 26.1 %copy-start.15 = (f32[1,32,32]{2,1,0:T(8,128)S(1)}, f32[1,32,32]{2,1,0:T(8,128)}, u32[]{:S(2)}) copy-start(f32[1,32,32]{2,1,0:T(8,128)} %param.35) | copy-start | bytes 12292
  622.8 23.7 %collective-permute-start = (bf16[160,3072]{1,0:T(8,128)(2,1)}, bf16[160,3072]{1,0:T(8,128)(2,1)}, u32[]{:S(2)}, u32[]{:S(2)}) collective-permute-start(bf16[160,3072]{1,0:T(8,128)(2,1)} %pad_maximum_fusion.2), channel_id=1, source_target_pairs={{16,0},{0,16},{17,1},{1,17},{18,2},{2,18},{19,3},{3,19},{20,4},{4,... | collective-permute-start | bytes 2949128 | tf_op jit(solution)/shard_map/ppermute | solution.py:17
Sparse Core Ops, SparseCore 0:
  69.5 36.1 all-gather.5
  107.9 62.3 all-gather.9
  171.9 164.7 all-gather.7
  338.6 115.0 all-gather.11
  473.1 85.1 all-gather.13
  571.7 47.7 reduce-scatter.1
where the time goes:
time: 661 us; the launch traced here: 659 us
  waiting for transfers between devices  403 us (61%)
  blocking collectives  97.8 us (15%)
  matrix products  60.7 us (9%)
  local copies, waits for them, and re-layouts  31.1 us (5%)
  other arithmetic  30.3 us (5%)
  between operations  23.6 us (4%)
  starting transfers between devices  12.7 us (2%)
    all_gather x1, waiting for transfers between devices, shards(): piece = lax.all_gather(fresh_text, 'tok', axis=0, tiled=True)  108 us
    all_to_all x1, waiting for transfers between devices, shards(): lax.all_to_all(text_cols, 'tok', split_axis=0, concat_axis=1, tiled=True)  104 us
    all_gather x1, waiting for transfers between devices, shards(): lax.all_gather(text_normed, 'tok', axis=0, tiled=True)  60.6 us
    reduce_scatter x1, waiting for transfers between devices, shards(): lax.psum_scatter(jnp.dot(hidden, down_weight, preferred_element_type=jnp....  35.7 us
    all_gather x1, waiting for transfers between devices, shards(): patch_rows = lax.all_gather(fresh_image, 'tok', axis=0, tiled=True)  31.7 us
    all_gather x1, blocking collectives, shards(): lax.all_gather(mlp_normed, 'tok', axis=0, tiled=True)  30.4 us
    all_gather x1, waiting for transfers between devices, shards(): piece = lax.all_gather(current, 'tok', axis=0, tiled=True)  29.7 us
    all_gather x1, blocking collectives, shards(): lax.all_gather(attended[:image_rows], 'tok', axis=0, tiled=True)  24.8 us
  transfers between devices with their start and end apart: 10, of which 9 were waited for; matrix products, arithmetic and copies ran while one was open for 12% of the time, Pallas kernels for 0%

commit v1 on v0

--- a/solution.py
+++ b/solution.py
@@ -1,10 +1,13 @@
 import jax
 import jax.numpy as jnp
 from jax import lax
+from jax.experimental import pallas as pl
+from jax.experimental.pallas import tpu as pltpu
 from jax.sharding import PartitionSpec as P
 
 HDIM = 128
 TSTEPS = 4
+PATCHES = 4
 
 
 eps = 1e-06
@@ -209,6 +212,224 @@
     return (image_next[None, None], text_next[None, None], current[None, None], latents_next[None])
 
 
+def unit_rms(block, gain):
+    power = jnp.mean(block * block, axis=-1, keepdims=True)
+    return (block * lax.rsqrt(power + eps) * gain).astype(jnp.bfloat16)
+
+
+def head_kernel(
+    patch_ref, count_ref, q_ref, k_ref, v_ref, ks_ref, vs_ref, gain_ref, out_ref, keys, values
+):
+    cache_rows = ks_ref.shape[0]
+    rows = k_ref.shape[0]
+    image_rows = rows - (keys.shape[0] - cache_rows)
+    text_rows = rows - image_rows
+    gains = gain_ref[...]
+    f32 = jnp.float32
+    begin = pl.multiple_of(patch_ref[0] * image_rows, image_rows)
+    keys[pl.ds(0, cache_rows), :] = ks_ref[...]
+    values[pl.ds(0, cache_rows), :] = vs_ref[...]
+    keys[pl.ds(begin, image_rows), :] = unit_rms(k_ref[pl.ds(0, image_rows), :].astype(f32), gains[1:2])
+    values[pl.ds(begin, image_rows), :] = v_ref[pl.ds(0, image_rows), :]
+    keys[pl.ds(cache_rows, text_rows), :] = unit_rms(
+        k_ref[pl.ds(image_rows, text_rows), :].astype(f32), gains[3:4]
+    )
+    values[pl.ds(cache_rows, text_rows), :] = v_ref[pl.ds(image_rows, text_rows), :]
+    all_keys = keys[...]
+    all_values = values[...]
+    column = lax.broadcasted_iota(jnp.int32, (1, cache_rows + text_rows), 1)
+    valid = column < cache_rows + count_ref[0]
+    chunk = image_rows
+    for part in range(rows // chunk):
+        span = pl.ds(part * chunk, chunk)
+        gain = gains[0:1] if part == 0 else gains[2:3]
+        query = unit_rms(q_ref[span, :].astype(f32), gain)
+        scores = lax.dot_general(
+            query, all_keys, (((1,), (1,)), ((), ())), preferred_element_type=f32
+        ) * HDIM ** (-0.5)
+        scores = jnp.where(valid, scores, masked_score)
+        highest = jnp.max(scores, axis=-1, keepdims=True)
+        expo = jnp.exp(scores - highest)
+        total = jnp.sum(expo, axis=-1, keepdims=True)
+        mixed = jnp.dot(expo.astype(jnp.bfloat16), all_values, preferred_element_type=f32)
+        out_ref[span, :] = (mixed / total).astype(jnp.bfloat16)
+
+
+def head_attention(patch, count, q, k, v, stale_k, stale_v, gains):
+    rows, width = q.shape
+    cache_rows = stale_k.shape[0]
+    image_rows = patch_rows_of(cache_rows)
+    total_keys = cache_rows + rows - image_rows
+    tall = pl.BlockSpec((rows, HDIM), lambda h, *_: (0, h))
+    kept = pl.BlockSpec((cache_rows, HDIM), lambda h, *_: (0, h))
+    return pl.pallas_call(
+        head_kernel,
+        out_shape=jax.ShapeDtypeStruct((rows, width), jnp.bfloat16),
+        grid_spec=pltpu.PrefetchScalarGridSpec(
+            num_scalar_prefetch=2,
+            grid=(width // HDIM,),
+            in_specs=[
+                tall,
+                tall,
+                tall,
+                kept,
+                kept,
+                pl.BlockSpec((4, HDIM), lambda h, *_: (0, 0)),
+            ],
+            out_specs=tall,
+            scratch_shapes=[
+                pltpu.VMEM((total_keys, HDIM), jnp.bfloat16),
+                pltpu.VMEM((total_keys, HDIM), jnp.bfloat16),
+            ],
+        ),
+        compiler_params=pltpu.CompilerParams(vmem_limit_bytes=32 * 1024 * 1024),
+        cost_estimate=pl.CostEstimate(
+            flops=4 * rows * total_keys * width,
+            bytes_accessed=2 * width * (4 * rows + 2 * cache_rows),
+            transcendentals=rows * total_keys * (width // HDIM),
+        ),
+    )(patch[None], count[None], q, k, v, stale_k, stale_v, gains)
+
+
+def patch_rows_of(cache_rows):
+    return cache_rows // PATCHES
+
+
+def swap_heads(cols, position):
+    count = lax.axis_size("tok")
+    block = cols.shape[1] // 3
+    first, second, third = (cols[:, i * block : (i + 1) * block] for i in range(3))
+    even = position % 2 == 0
+    near = lax.ppermute(second, "tok", [(0, 1), (1, 0), (2, 3), (3, 2)])
+    far = lax.ppermute(
+        jnp.where(even, third, first), "tok", [(0, 2), (2, 0), (1, 3), (3, 1)]
+    )
+    stay = jnp.where(even, first, third)
+    query = jnp.where(position == 0, stay, jnp.where(position == 1, near, far))
+    key = jnp.where((position == 0) | (position == 3), near, stay)
+    value = jnp.where(position == 3, stay, jnp.where(position == 2, near, far))
+    return query, key, value
+
+
+def shards_by_head(
+    image_in,
+    text_in,
+    text_length,
+    entry_order,
+    step_index,
+    image_modulation,
+    text_modulation,
+    image_to_heads,
+    text_to_heads,
+    head_gain,
+    image_from_heads,
+    text_from_heads,
+    image_up,
+    image_down,
+    stale_cache,
+    final_modulation,
+    final_weight,
+    latents,
+):
+    f32, bf16 = jnp.float32, jnp.bfloat16
+    section = lax.axis_index("section")
+    last_section = lax.axis_size("section") - 1
+    position = lax.axis_index("tok")
+    count = lax.axis_size("tok")
+    text_x = text_in[0, 0].astype(f32)
+    image_rows, width = image_in.shape[2:]
+    text_rows = text_in.shape[2]
+    patch_len = image_rows * count
+    share = width // count
+    patch = lax.dynamic_index_in_dim(entry_order[0], section, 0, False)
+    step_now = lax.dynamic_index_in_dim(step_index[0], patch, 0, False)
+    modul = (
+        lax.dynamic_index_in_dim(image_modulation[0], step_now, 0, False)
+        .astype(f32)
+        .reshape(6, width)
+    )
+    text_mod = (
+        lax.dynamic_index_in_dim(text_modulation[0], step_now, 0, False)
+        .astype(f32)
+        .reshape(3, width)
+    )
+    stale = stale_cache[0, 0]
+    cache_rows = stale.shape[0]
+    stale_heads = lax.all_to_all(
+        stale.reshape(cache_rows, 2, count, share), "tok", split_axis=2, concat_axis=0, tiled=False
+    )
+    stale_k = stale_heads[:, :, 0].reshape(count * cache_rows, share)
+    stale_v = stale_heads[:, :, 1].reshape(count * cache_rows, share)
+    text_normed = modulate(text_x, text_mod[0], text_mod[1]).astype(bf16)
+    own = jnp.concatenate([image_in[0, 0], text_normed], axis=0)
+    every = lax.all_gather(own, "tok", axis=0, tiled=False)
+    every_image_x = every[:, :image_rows].reshape(patch_len, width).astype(f32)
+    every_text = every[:, image_rows:].reshape(count * text_rows, width)
+    every_image = modulate(every_image_x, modul[0], modul[1]).astype(bf16)
+    image_cols = jnp.dot(every_image, image_to_heads[0], preferred_element_type=f32).astype(bf16)
+    text_cols = jnp.dot(every_text, text_to_heads[0], preferred_element_type=f32).astype(bf16)
+    query, key, value = swap_heads(jnp.concatenate([image_cols, text_cols], axis=0), position)
+    gains = head_gain[0]
+    image_key = head_norm(key[:patch_len].astype(f32), gains[1]).astype(bf16)
+    attended = head_attention(patch, text_length[0], query, key, value, stale_k, stale_v, gains)
+    fresh = lax.all_gather(
+        jnp.stack([image_key, value[:patch_len]], axis=0), "tok", axis=0, tiled=False
+    )
+    patch_rows = fresh.transpose(2, 1, 0, 3).reshape(patch_len, 2 * width)
+    first_row = position * cache_rows
+    begin = patch * patch_len
+    offset = jnp.clip(first_row - begin, 0, patch_len - cache_rows)
+    window = lax.dynamic_slice_in_dim(patch_rows, offset, cache_rows, 0)
+    inside = jnp.logical_and(first_row >= begin, first_row < begin + patch_len)
+    current = jnp.where(inside, window, stale)
+    every_att = lax.all_gather(attended, "tok", axis=0, tiled=False)
+    image_back_cols = jnp.einsum(
+        "trd,tdc->rc",
+        every_att[:, :patch_len],
+        image_from_heads[0].reshape(count, share, share),
+        preferred_element_type=f32,
+    ).astype(bf16)
+    text_back_cols = jnp.einsum(
+        "trd,tdc->rc",
+        every_att[:, patch_len:],
+        text_from_heads[0].reshape(count, share, share),
+        preferred_element_type=f32,
+    ).astype(bf16)
+    image_back = lax.all_gather(image_back_cols, "tok", axis=1, tiled=True)
+    text_back = lax.all_to_all(text_back_cols, "tok", split_axis=0, concat_axis=1, tiled=True)
+    image_mid = every_image_x + modul[2] * image_back.astype(f32)
+    text_out = (text_x + text_mod[2] * text_back.astype(f32)).astype(bf16)
+    text_next = from_behind(text_out, "section", 1)
+    mlp_normed = modulate(image_mid, modul[3], modul[4]).astype(bf16)
+    hidden = jax.nn.gelu(
+        jnp.dot(mlp_normed, image_up[0], preferred_element_type=f32), approximate=True
+    ).astype(bf16)
+    partial = jnp.dot(hidden, image_down[0], preferred_element_type=f32)
+    parts = lax.all_to_all(
+        partial.astype(bf16).reshape(count, image_rows, width),
+        "tok",
+        split_axis=0,
+        concat_axis=0,
+        tiled=False,
+    )
+    reduced = jnp.sum(parts.astype(f32), axis=0)
+    mid_own = lax.dynamic_slice_in_dim(image_mid, position * image_rows, image_rows, 0)
+    image_out = (mid_own + modul[5] * reduced).astype(bf16)
+    image_next = from_behind(image_out, "section", 1)
+    final_source = jnp.where(section == last_section, image_out, image_next)
+    patch_last = entry_order[0, last_section]
+    step_last = lax.dynamic_index_in_dim(step_index[0], patch_last, 0, False)
+    final_mod = (
+        lax.dynamic_index_in_dim(final_modulation, step_last, 0, False)
+        .astype(f32)
+        .reshape(2, width)
+    )
+    normed = modulate(final_source.astype(f32), final_mod[0], final_mod[1]).astype(bf16)
+    velocity = jnp.dot(normed, final_weight, preferred_element_type=f32)
+    latents_next = latents[0] + -1.0 / TSTEPS * velocity
+    return (image_next[None, None], text_next[None, None], current[None, None], latents_next[None])
+
+
 def solution(mesh):
     placed = (
         P("section", "grp", "tok", None),
@@ -231,7 +452,7 @@
         P("grp", "tok", "section"),
     )
     return jax.shard_map(
-        shards,
+        shards_by_head if mesh.shape["tok"] == 4 else shards,
         mesh=mesh,
         in_specs=placed,
         out_specs=(

time: 661 us -> 421 us (0.64)
  waiting for transfers between devices: 403 us -> 245 us
  blocking collectives: 97.8 us -> 26.4 us
  matrix products: 60.7 us -> 44.1 us
  Pallas kernels: 0 us -> 14.5 us
  local copies, waits for them, and re-layouts: 31.1 us -> 22.9 us
  starting transfers between devices: 12.7 us -> 20.1 us
  other arithmetic: 30.3 us -> 23.5 us
    all_to_all x3, waiting for transfers between devices: 117 us -> 17.9 us  [the longest x1 14.5 us: shards_by_head(): lax.all_to_all(text_back_cols, 'tok', split_axis=0, concat_axis=1, tiled=...]
    all_gather x5 -> x3, waiting for transfers between devices: 230 us -> 168 us  [the longest x1 100 us: shards_by_head(): every = lax.all_gather(own, 'tok', axis=0, tiled=False)]
    all_gather x3 -> x1, blocking collectives: 76.5 us -> 26.4 us  [shards_by_head(): image_back = lax.all_gather(image_back_cols, 'tok', axis=1, tiled=True)]
    ppermute x0 -> x2, waiting for transfers between devices: none -> 43.3 us  [the longest x1 41.1 us: swap_heads(): near = lax.ppermute(second, 'tok', [(0, 1), (1, 0), (2, 3), (3, 2)])]
    reduce_scatter x1 -> x0, waiting for transfers between devices: 35.7 us -> none  [shards(): lax.psum_scatter(jnp.dot(hidden, down_weight, preferred_element_type=jnp....]
    all_to_all x1 -> x0, blocking collectives: 21.3 us -> none  [shards(): lax.all_to_all(image_back_cols, 'tok', split_axis=0, concat_axis=1, tiled...]
    dot_general x10 -> x6, matrix products: 60.7 us -> 44.1 us  [the longest x1 18.2 us: shards_by_head(): partial = jnp.dot(hidden, image_down[0], preferred_element_type=f32)]
    pallas_call x0 -> x1, Pallas kernels: none -> 14.5 us  [head_attention(): pl.pallas_call(head_kernel, out_shape=jax.ShapeDtypeStruct((rows, width),...]
  transfers between devices with their start and end apart: 10 -> 10, of which waited for: 9 -> 7; matrix products, arithmetic and copies ran while one was open for 12% -> 18% of each run, Pallas kernels for 0% -> 0%
where the time goes in v1:
time: 421 us; the launch traced here: 420 us
  waiting for transfers between devices  245 us (58%)
  matrix products  44.1 us (10%)
  blocking collectives  26.4 us (6%)
  other arithmetic  23.5 us (6%)
  between operations  23.2 us (6%)
  local copies, waits for them, and re-layouts  22.9 us (5%)
  starting transfers between devices  20.1 us (5%)
  Pallas kernels  14.5 us (3%)
    all_gather x1, waiting for transfers between devices, shards_by_head(): every = lax.all_gather(own, 'tok', axis=0, tiled=False)  100 us
    all_gather x1, waiting for transfers between devices, shards_by_head(): every_att = lax.all_gather(attended, 'tok', axis=0, tiled=False)  68 us
    ppermute x1, waiting for transfers between devices, swap_heads(): near = lax.ppermute(second, 'tok', [(0, 1), (1, 0), (2, 3), (3, 2)])  41.1 us
    all_gather x1, blocking collectives, shards_by_head(): image_back = lax.all_gather(image_back_cols, 'tok', axis=1, tiled=True)  26.4 us
    dot_general x1, matrix products, shards_by_head(): partial = jnp.dot(hidden, image_down[0], preferred_element_type=f32)  18.2 us
    ppermute x2, waiting for transfers between devices, from_behind(): return lax.ppermute(block, axis, route)  15.4 us
    all_to_all x1, waiting for transfers between devices, shards_by_head(): lax.all_to_all(text_back_cols, 'tok', split_axis=0, concat_axis=1, tiled=...  14.5 us
    pallas_call x1, Pallas kernels, head_attention(): pl.pallas_call(head_kernel, out_shape=jax.ShapeDtypeStruct((rows, width),...  14.5 us
  transfers between devices with their start and end apart: 10, of which 7 were waited for; matrix products, arithmetic and copies ran while one was open for 18% of the time, Pallas kernels for 0%

profile of v1, /device:TPU:0, one launch (start us, length us, event | category | flops | bytes accessed | tf_op | source)
XLA Modules:
  0.0 419.8 jit_solution(18072448447093992286)
XLA Ops:
  7.2 1.3 fusion.76
  12.5 1.3 constant_dynamic-slice_fusion
  15.7 0.9 dynamic-slice_convert_fusion.1
  16.7 1.4 convert_reduce_fusion
  18.1 1.5 fusion.23
  20.0 1.0 pad_maximum_fusion.1
  21.0 0.7 copy-done.5
  21.7 1.6 copy.34
  23.3 2.6 copy.35
  25.9 6.4 %all-to-all-start = ((bf16[1,128,2,4,768]{4,1,2,0,3:T(8,128)(2,1)}), bf16[1,128,2,4,768]{4,1,2,0,3:T(8,128)(2,1)S(1)}, u32[]{:S(2)}, u32[]{:S(2)}) async-start(bf16[1,128,2,4,768]{4,1,2,0,3:T(8,128)(2,1)} %copy.35), calls=%async_computation | async-start | bytes 3145728 | tf_op jit(solution)/shard_map/all_to_all | solution.py:358
  32.4 100.4 %all-gather.7.cloned.1.call-done = bf16[640,3072]{1,0:T(8,128)(2,1)} async-done(((bf16[160,3072]{1,0:T(8,128)(2,1)}), bf16[640,3072]{1,0:T(8,128)(2,1)}) %all-gather.7.cloned.1.call-update) | async-done | bytes 3932176 | tf_op jit(solution)/shard_map/all_gather | solution.py:365
  132.9 1.3 convert_reduce_fusion.2
  134.2 2.3 slice.146
  136.5 1.5 multiply_reduce_fusion.1
  138.0 1.7 add_convert_fusion.1
  139.7 7.2 %fusion.14 = bf16[128,2304]{1,0:T(8,128)(2,1)S(1)} fusion(bf16[128,3072]{1,0:T(8,128)(2,1)S(1)} %bitcast.127, bf16[1,3072,2304]{2,1,0:T(8,128)(2,1)} %param.25), kind=kOutput, calls=%fused_computation.12 | convolution fusion | flops 1812234240 | bytes 15532032 | tf_op jit(solution)/shard_map/dot_general | solution.py:369
  147.0 7.7 %fusion.8 = bf16[512,2304]{1,0:T(8,128)(2,1)S(1)} fusion(bf16[512,3072]{1,0:T(8,128)(2,1)S(1)} %bitcast.128, bf16[1,3072,2304]{2,1,0:T(8,128)(2,1)S(1)} %bitcast.151), kind=kOutput, calls=%fused_computation.8 | convolution fusion | flops 7248936960 | bytes 19660800 | tf_op jit(solution)/shard_map/dot_general | solution.py:370
  154.7 1.8 broadcast_select_fusion.2
  156.9 2.0 collective-permute-start.1
  159.6 41.1 %collective-permute-done = bf16[640,768]{1,0:T(8,128)(2,1)} collective-permute-done((bf16[640,768]{1,0:T(8,128)(2,1)}, bf16[640,768]{1,0:T(8,128)(2,1)}, u32[]{:S(2)}, u32[]{:S(2)}) %collective-permute-start) | collective-permute-done | bytes 983072 | tf_op jit(solution)/shard_map/ppermute | solution.py:303
  200.8 2.1 collective-permute-done.1
  202.9 1.8 select_select_fusion
  204.7 1.7 broadcast_select_fusion.1
  206.4 14.5 %shard_map.201 = bf16[640,768]{1,0:T(8,128)(2,1)} custom-call(s32[1]{0:T(128)} %bitcast.9.patch_ref, s32[1]{0:T(128)S(6)} %copy.43.count_ref, bf16[640,768]{1,0:T(8,128)(2,1)S(1)} %get-tuple-element.13.q_ref, bf16[640,768]{1,0:T(8,128)(2,1)S(1)} %get-tuple-element.12.k_ref, bf16[640,768]{1,0:T(8,128)(2,1)S(1)} %get-tuple-element.8.v_ref, ...), custom_call_target="tpu_custom_call" | custom-call | flops 2013265920 | bytes 5505024 | tf_op jit(solution)/shard_map/pallas_call | solution.py:265
  223.8 0.8 convert_multiply_fusion.1
  224.6 1.1 copy.37
  225.8 0.8 mul.204
  226.6 1.2 copy.38
  227.9 0.8 pad_maximum_fusion.2
  228.7 68.0 %all-gather.9.cloned.1.call-done = bf16[2560,768]{1,0:T(8,128)(2,1)} async-done(((bf16[640,768]{1,0:T(8,128)(2,1)}), bf16[2560,768]{1,0:T(8,128)(2,1)}) %all-gather.9.cloned.1.call-update) | async-done | bytes 3932176 | tf_op jit(solution)/shard_map/all_gather | solution.py:385
  296.7 3.4 fusion.42
  300.1 26.4 %all_gather.25 = bf16[128,3072]{1,0:T(8,128)(2,1)S(1)} all-gather(bf16[128,768]{1,0:T(8,128)(2,1)S(1)} %fusion.42), channel_id=1, replica_groups=mesh['section'=2,'grp'=4,'tok'=4] {'tok'}, dimensions={1}, use_global_device_ids=true | all-gather | bytes 983040 | tf_op jit(solution)/shard_map/all_gather | solution.py:398
  326.4 1.5 fusion.72
  328.2 18.2 %fusion.11 = bf16[128,3072]{1,0:T(8,128)(2,1)} fusion(bf16[1,3072,3072]{2,1,0:T(8,128)(2,1)} %param.31, bf16[1,3072,3072]{2,1,0:T(8,128)(2,1)} %param.30, f32[128,3072]{1,0:T(8,128)S(1)} %get-tuple-element.7, f32[3072]{0:T(1024)S(1)} %bitcast.146, f32[3072]{0:T(1024)S(1)} %bitcast.147, f32[128]{0:T(128)S(1)} %add_rsqrt_fusion.3, ...), kind=kOutput, calls=%fused_computation.11 | convolution fusion | flops 4837736448 | bytes 40133632 | tf_op jit(solution)/shard_map/dot_general | solution.py:407
  346.4 3.5 all-to-all-start.1
  349.9 3.8 copy.39
  353.7 4.0 reshape.194
  357.7 6.8 %bitcast_convert_fusion = bf16[512,768]{1,0:T(8,128)(2,1)} fusion(bf16[4,768,768]{2,1,0:T(8,128)(2,1)} %bitcast.152, bf16[4,640,768]{2,1,0:T(8,128)(2,1)} %bitcast.137), kind=kOutput, calls=%fused_computation.37 | convolution fusion | flops 2416312320 | bytes 8650752 | tf_op jit(solution)/shard_map/trd,tdc->rc/dot_general | solution.py:392
  364.5 3.4 all-to-all-done.1
  367.8 4.2 %all-to-all-start.2 = ((bf16[4,128,768]{2,1,0:T(8,128)(2,1)}), bf16[4,128,768]{2,1,0:T(8,128)(2,1)}, u32[]{:S(2)}, u32[]{:S(2)}) async-start(bf16[4,128,768]{2,1,0:T(8,128)(2,1)} %bitcast.133), calls=%async_computation.2 | async-start | bytes 1572864 | tf_op jit(solution)/shard_map/all_to_all | solution.py:399
  372.1 2.7 broadcast_select_fusion
  374.9 1.8 collective-permute-start.2
  376.7 14.5 %all-to-all-done.2 = bf16[4,128,768]{2,1,0:T(8,128)(2,1)} async-done(((bf16[4,128,768]{2,1,0:T(8,128)(2,1)}), bf16[4,128,768]{2,1,0:T(8,128)(2,1)}, u32[]{:S(2)}, u32[]{:S(2)}) %all-to-all-start.2) | async-done | bytes 786464 | tf_op jit(solution)/shard_map/all_to_all | solution.py:399
  391.3 1.3 convert_bitcast_fusion.1
  392.9 2.0 collective-permute-start.3
  395.4 0.9 fusion.44
  396.3 15.4 %collective-permute-done.3 = bf16[128,3072]{1,0:T(8,128)(2,1)S(1)} collective-permute-done((bf16[128,3072]{1,0:T(8,128)(2,1)S(1)}, bf16[128,3072]{1,0:T(8,128)(2,1)S(1)}, u32[]{:S(2)}, u32[]{:S(2)}) %collective-permute-start.3) | collective-permute-done | bytes 786464 | tf_op jit(solution)/shard_map/ppermute | solution.py:20
  412.4 0.9 copy.45
  (67 shorter events, 3.5 us)
Async XLA Ops:
  7.2 388.2 %copy-start = (bf16[3072,32]{0,1:T(8,128)(2,1)S(1)}, bf16[3072,32]{0,1:T(8,128)(2,1)}, u32[]{:S(2)}) copy-start(bf16[3072,32]{0,1:T(8,128)(2,1)} %param.34) | copy-start | bytes 589828
  7.2 12.4 %copy-start.2 = (bf16[1,1,128,3072]{3,2,1,0:T(8,128)(2,1)S(1)}, bf16[1,1,128,3072]{3,2,1,0:T(8,128)(2,1)}, u32[]{:S(2)}) copy-start(bf16[1,1,128,3072]{3,2,1,0:T(8,128)(2,1)} %param.19) | copy-start | bytes 2359300
  7.2 125.7 %all-gather.7.cloned.1.call-start = ((), (), s32[]{:S(2)}) async-start(), calls=%async_computation.3 | async-start | bytes 4915200 | tf_op jit(solution)/shard_map/all_gather | solution.py:365
  16.7 3.3 copy-start.6
  20.0 1.8 copy-start.5
  25.9 6.5 %copy-start.7 = (bf16[1,4,18432]{2,1,0:T(4,128)(2,1)S(1)}, bf16[1,4,18432]{2,1,0:T(4,128)(2,1)}, u32[]{:S(2)}) copy-start(bf16[1,4,18432]{2,1,0:T(4,128)(2,1)} %param.23) | copy-start | bytes 442372
  25.9 133.6 %all-to-all-start = ((bf16[1,128,2,4,768]{4,1,2,0,3:T(8,128)(2,1)}), bf16[1,128,2,4,768]{4,1,2,0,3:T(8,128)(2,1)S(1)}, u32[]{:S(2)}, u32[]{:S(2)}) async-start(bf16[1,128,2,4,768]{4,1,2,0,3:T(8,128)(2,1)} %copy.35), calls=%async_computation | async-start | bytes 3145728 | tf_op jit(solution)/shard_map/all_to_all | solution.py:358
  32.3 264.4 %all-gather.9.cloned.1.call-start = ((), (), s32[]{:S(2)}) async-start(), calls=%async_computation.4 | async-start | bytes 4915200 | tf_op jit(solution)/shard_map/all_gather | solution.py:385
  134.2 12.7 %slice-start = ((s8[14155776]{0:T(1024)(128)(4,1)}), s8[4194304]{0:T(1024)(128)(4,1)S(1)}, s32[]{:S(2)}) async-start(s8[14155776]{0:T(1024)(128)(4,1)} %bitcast.150), calls=%async_computation.6 | async-start | bytes 8388608
  138.0 8.9 %slice-start.1 = ((s8[14155776]{0:T(1024)(128)(4,1)}), s8[4194304]{0:T(1024)(128)(4,1)S(1)}, s32[]{:S(2)}) async-start(s8[14155776]{0:T(1024)(128)(4,1)} %bitcast.150), calls=%async_computation.7 | async-start | bytes 8388608
  139.7 7.3 %slice-start.2 = ((s8[14155776]{0:T(1024)(128)(4,1)}), s8[4194304]{0:T(1024)(128)(4,1)S(1)}, s32[]{:S(2)}) async-start(s8[14155776]{0:T(1024)(128)(4,1)} %bitcast.150), calls=%async_computation.8 | async-start | bytes 8388608
  139.7 7.3 %slice-start.3 = ((s8[14155776]{0:T(1024)(128)(4,1)}), s8[1572864]{0:T(1024)(128)(4,1)S(1)}, s32[]{:S(2)}) async-start(s8[14155776]{0:T(1024)(128)(4,1)} %bitcast.150), calls=%async_computation.9 | async-start | bytes 3145728
  154.7 2.2 copy-start.3
  156.9 43.9 %collective-permute-start = (bf16[640,768]{1,0:T(8,128)(2,1)}, bf16[640,768]{1,0:T(8,128)(2,1)}, u32[]{:S(2)}, u32[]{:S(2)}) collective-permute-start(bf16[640,768]{1,0:T(8,128)(2,1)} %get-tuple-element.11), channel_id=1, source_target_pairs={{0,1},{1,0},{2,3},{3,2},{4,5},{5,4},{6,7},{7,6},{8,9},{9,8},{10,11... | collective-permute-start | bytes 2949128 | tf_op jit(solution)/shard_map/ppermute | solution.py:303
  156.9 46.0 %collective-permute-start.1 = (bf16[640,768]{1,0:T(8,128)(2,1)}, bf16[640,768]{1,0:T(8,128)(2,1)}, u32[]{:S(2)}, u32[]{:S(2)}) collective-permute-start(bf16[640,768]{1,0:T(8,128)(2,1)} %get-tuple-element.10), channel_id=1, source_target_pairs={{0,2},{2,0},{1,3},{3,1},{4,6},{6,4},{5,7},{7,5},{8,10},{10,8},{9,1... | collective-permute-start | bytes 2949128 | tf_op jit(solution)/shard_map/ppermute | solution.py:304
  159.5 43.4 %copy-start.4 = (bf16[512,2304]{1,0:T(8,128)(2,1)S(1)}, bf16[512,2304]{1,0:T(8,128)(2,1)}, u32[]{:S(2)}) copy-start(bf16[512,2304]{1,0:T(8,128)(2,1)} %copy-done.3) | copy-start | bytes 7077892
  204.7 1.7 copy-start.1
  206.4 17.4 %copy-start.8 = (bf16[4,6144]{1,0:T(4,128)(2,1)S(1)}, bf16[4,6144]{1,0:T(4,128)(2,1)}, u32[]{:S(2)}) copy-start(bf16[4,6144]{1,0:T(4,128)(2,1)} %param.33) | copy-start | bytes 147460
  220.9 129.0 %all-gather.11.cloned.1.call-start = ((), (), s32[]{:S(2)}) async-start(), calls=%async_computation.5 | async-start | bytes 1966080 | tf_op jit(solution)/shard_map/all_gather | solution.py:375
  346.4 21.4 %all-to-all-start.1 = ((bf16[4,32,3072]{2,1,0:T(8,128)(2,1)}), bf16[4,32,3072]{2,1,0:T(8,128)(2,1)S(1)}, u32[]{:S(2)}, u32[]{:S(2)}) async-start(bf16[4,32,3072]{2,1,0:T(8,128)(2,1)} %bitcast.134), calls=%async_computation.1 | async-start | bytes 1572864 | tf_op jit(solution)/shard_map/all_to_all | solution.py:408
  367.8 23.4 %all-to-all-start.2 = ((bf16[4,128,768]{2,1,0:T(8,128)(2,1)}), bf16[4,128,768]{2,1,0:T(8,128)(2,1)}, u32[]{:S(2)}, u32[]{:S(2)}) async-start(bf16[4,128,768]{2,1,0:T(8,128)(2,1)} %bitcast.133), calls=%async_computation.2 | async-start | bytes 1572864 | tf_op jit(solution)/shard_map/all_to_all | solution.py:399
  374.9 20.0 %collective-permute-start.2 = (bf16[32,3072]{1,0:T(8,128)(2,1)S(1)}, bf16[32,3072]{1,0:T(8,128)(2,1)S(1)}, u32[]{:S(2)}, u32[]{:S(2)}) collective-permute-start(bf16[32,3072]{1,0:T(8,128)(2,1)S(1)} %add_convert_fusion.5), channel_id=1, source_target_pairs={{16,0},{0,16},{17,1},{1,17},{18,2},{2,18},{19,3},{3,19},{20,4},{4,... | collective-permute-start | bytes 589832 | tf_op jit(solution)/shard_map/ppermute | solution.py:20
  392.7 2.7 copy-start.9
  392.9 18.7 %collective-permute-start.3 = (bf16[128,3072]{1,0:T(8,128)(2,1)S(1)}, bf16[128,3072]{1,0:T(8,128)(2,1)S(1)}, u32[]{:S(2)}, u32[]{:S(2)}) collective-permute-start(bf16[128,3072]{1,0:T(8,128)(2,1)S(1)} %fusion.27), channel_id=1, source_target_pairs={{16,0},{0,16},{17,1},{1,17},{18,2},{2,18},{19,3},{3,19},{20,4},{4,... | collective-permute-start | bytes 2359304 | tf_op jit(solution)/shard_map/ppermute | solution.py:20
Sparse Core Ops, SparseCore 0:
  21.2 111.6 all-gather.6
  221.0 75.5 all-gather.8
  298.2 43.2 all-gather.10

commit v2 on v1

--- a/solution.py
+++ b/solution.py
@@ -355,14 +355,15 @@
     )
     stale = stale_cache[0, 0]
     cache_rows = stale.shape[0]
-    stale_heads = lax.all_to_all(
-        stale.reshape(cache_rows, 2, count, share), "tok", split_axis=2, concat_axis=0, tiled=False
-    )
-    stale_k = stale_heads[:, :, 0].reshape(count * cache_rows, share)
-    stale_v = stale_heads[:, :, 1].reshape(count * cache_rows, share)
     text_normed = modulate(text_x, text_mod[0], text_mod[1]).astype(bf16)
     own = jnp.concatenate([image_in[0, 0], text_normed], axis=0)
     every = lax.all_gather(own, "tok", axis=0, tiled=False)
+    every, late_stale = lax.optimization_barrier((every, stale))
+    stale_heads = lax.all_to_all(
+        late_stale.reshape(cache_rows, 2, count, share), "tok", split_axis=2, concat_axis=0, tiled=False
+    )
+    stale_k = stale_heads[:, :, 0].reshape(count * cache_rows, share)
+    stale_v = stale_heads[:, :, 1].reshape(count * cache_rows, share)
     every_image_x = every[:, :image_rows].reshape(patch_len, width).astype(f32)
     every_text = every[:, image_rows:].reshape(count * text_rows, width)
     every_image = modulate(every_image_x, modul[0], modul[1]).astype(bf16)
@@ -382,20 +383,17 @@
     window = lax.dynamic_slice_in_dim(patch_rows, offset, cache_rows, 0)
     inside = jnp.logical_and(first_row >= begin, first_row < begin + patch_len)
     current = jnp.where(inside, window, stale)
-    every_att = lax.all_gather(attended, "tok", axis=0, tiled=False)
-    image_back_cols = jnp.einsum(
-        "trd,tdc->rc",
-        every_att[:, :patch_len],
-        image_from_heads[0].reshape(count, share, share),
-        preferred_element_type=f32,
-    ).astype(bf16)
+    image_att = lax.all_gather(attended[:patch_len], "tok", axis=1, tiled=True)
+    image_att, text_own = lax.optimization_barrier((image_att, attended[patch_len:]))
+    text_att = lax.all_gather(text_own, "tok", axis=0, tiled=False)
+    image_back_cols = jnp.dot(image_att, image_from_heads[0], preferred_element_type=f32).astype(bf16)
+    image_back = lax.all_gather(image_back_cols, "tok", axis=1, tiled=True)
     text_back_cols = jnp.einsum(
         "trd,tdc->rc",
-        every_att[:, patch_len:],
+        text_att,
         text_from_heads[0].reshape(count, share, share),
         preferred_element_type=f32,
     ).astype(bf16)
-    image_back = lax.all_gather(image_back_cols, "tok", axis=1, tiled=True)
     text_back = lax.all_to_all(text_back_cols, "tok", split_axis=0, concat_axis=1, tiled=True)
     image_mid = every_image_x + modul[2] * image_back.astype(f32)
     text_out = (text_x + text_mod[2] * text_back.astype(f32)).astype(bf16)

time: 421 us -> 398 us (0.945)
  waiting for transfers between devices: 245 us -> 205 us
  blocking collectives: 26.4 us -> 42.6 us
    all_gather x1, waiting for transfers between devices: 68 us -> 25.8 us  [shards_by_head(): text_att = lax.all_gather(text_own, 'tok', axis=0, tiled=False)]
    all_to_all x1, waiting for transfers between devices: 0.01 us -> 25.2 us  [shards_by_head(): lax.all_to_all(late_stale.reshape(cache_rows, 2, count, share), 'tok', sp...]
    all_gather x1, waiting for transfers between devices: 100 us -> 76.3 us  [shards_by_head(): every = lax.all_gather(own, 'tok', axis=0, tiled=False)]
    all_gather x0 -> x1, blocking collectives: none -> 17.7 us  [shards_by_head(): image_att = lax.all_gather(attended[:patch_len], 'tok', axis=1, tiled=True)]
    ppermute x1, waiting for transfers between devices: 2.11 us -> 8.54 us  [swap_heads(): lax.ppermute(jnp.where(even, third, first), 'tok', [(0, 2), (2, 0), (1, 3...]
  transfers between devices with their start and end apart: 10 -> 10, of which waited for: 7 -> 7; matrix products, arithmetic and copies ran while one was open for 18% -> 15% of each run, Pallas kernels for 0% -> 3%
where the time goes in v2:
time: 398 us; the launch traced here: 397 us
  waiting for transfers between devices  205 us (52%)
  matrix products  44 us (11%)
  blocking collectives  42.6 us (11%)
  other arithmetic  25.2 us (6%)
  local copies, waits for them, and re-layouts  24.8 us (6%)
  between operations  22.9 us (6%)
  starting transfers between devices  18.1 us (5%)
  Pallas kernels  13.8 us (3%)
    all_gather x1, waiting for transfers between devices, shards_by_head(): every = lax.all_gather(own, 'tok', axis=0, tiled=False)  76.3 us
    ppermute x1, waiting for transfers between devices, swap_heads(): near = lax.ppermute(second, 'tok', [(0, 1), (1, 0), (2, 3), (3, 2)])  37.1 us
    all_gather x1, waiting for transfers between devices, shards_by_head(): text_att = lax.all_gather(text_own, 'tok', axis=0, tiled=False)  25.8 us
    all_to_all x1, waiting for transfers between devices, shards_by_head(): lax.all_to_all(late_stale.reshape(cache_rows, 2, count, share), 'tok', sp...  25.2 us
    all_gather x1, blocking collectives, shards_by_head(): image_back = lax.all_gather(image_back_cols, 'tok', axis=1, tiled=True)  24.9 us
    dot_general x1, matrix products, shards_by_head(): partial = jnp.dot(hidden, image_down[0], preferred_element_type=f32)  18.2 us
    all_gather x1, blocking collectives, shards_by_head(): image_att = lax.all_gather(attended[:patch_len], 'tok', axis=1, tiled=True)  17.7 us
    all_to_all x1, waiting for transfers between devices, shards_by_head(): lax.all_to_all(text_back_cols, 'tok', split_axis=0, concat_axis=1, tiled=...  16.5 us
  transfers between devices with their start and end apart: 10, of which 7 were waited for; matrix products, arithmetic and copies ran while one was open for 15% of the time, Pallas kernels for 3%

profile of v2, /device:TPU:0, one launch (start us, length us, event | category | flops | bytes accessed | tf_op | source)
XLA Modules:
  0.0 396.9 jit_solution(11355597754073154251)
XLA Ops:
  7.2 1.3 fusion.75
  12.2 1.4 constant_dynamic-slice_fusion
  15.5 0.9 dynamic-slice_convert_fusion.1
  16.5 1.4 convert_reduce_fusion
  17.8 1.5 fusion.23
  19.7 1.0 pad_maximum_fusion.1
  21.5 1.6 copy.34
  23.8 76.3 %all-gather.7.cloned.1.call-done = bf16[640,3072]{1,0:T(8,128)(2,1)} async-done(((bf16[160,3072]{1,0:T(8,128)(2,1)}), bf16[640,3072]{1,0:T(8,128)(2,1)}) %all-gather.7.cloned.1.call-update) | async-done | bytes 3932176 | tf_op jit(solution)/shard_map/all_gather | solution.py:360
  100.1 1.3 convert_reduce_fusion.2
  101.4 2.3 slice.118
  103.7 1.5 multiply_reduce_fusion.1
  105.2 1.7 add_convert_fusion.1
  106.9 7.2 %fusion.16 = bf16[128,2304]{1,0:T(8,128)(2,1)S(1)} fusion(bf16[128,3072]{1,0:T(8,128)(2,1)S(1)} %bitcast.127, bf16[1,3072,2304]{2,1,0:T(8,128)(2,1)} %param.25), kind=kOutput, calls=%fused_computation.14 | convolution fusion | flops 1812234240 | bytes 15532032 | tf_op jit(solution)/shard_map/dot_general | solution.py:370
  114.2 7.7 %fusion.10 = bf16[512,2304]{1,0:T(8,128)(2,1)S(1)} fusion(bf16[512,3072]{1,0:T(8,128)(2,1)S(1)} %bitcast.128, bf16[1,3072,2304]{2,1,0:T(8,128)(2,1)S(1)} %bitcast.148), kind=kOutput, calls=%fused_computation.10 | convolution fusion | flops 7248936960 | bytes 19660800 | tf_op jit(solution)/shard_map/dot_general | solution.py:371
  122.0 1.6 broadcast_select_fusion.2
  123.5 1.2 collective-permute-start.1
  125.3 2.6 copy.35
  127.9 4.5 %all-to-all-start = ((bf16[1,128,2,4,768]{4,1,2,0,3:T(8,128)(2,1)}), bf16[1,128,2,4,768]{4,1,2,0,3:T(8,128)(2,1)}, u32[]{:S(2)}, u32[]{:S(2)}) async-start(bf16[1,128,2,4,768]{4,1,2,0,3:T(8,128)(2,1)} %copy.35), calls=%async_computation | async-start | bytes 3145728 | tf_op jit(solution)/shard_map/all_to_all | solution.py:362
  132.4 37.1 %collective-permute-done = bf16[640,768]{1,0:T(8,128)(2,1)S(1)} collective-permute-done((bf16[640,768]{1,0:T(8,128)(2,1)}, bf16[640,768]{1,0:T(8,128)(2,1)S(1)}, u32[]{:S(2)}, u32[]{:S(2)}) %collective-permute-start) | collective-permute-done | bytes 983072 | tf_op jit(solution)/shard_map/ppermute | solution.py:303
  169.4 0.9 copy-done.7
  170.4 8.5 %collective-permute-done.1 = bf16[640,768]{1,0:T(8,128)(2,1)} collective-permute-done((bf16[640,768]{1,0:T(8,128)(2,1)}, bf16[640,768]{1,0:T(8,128)(2,1)}, u32[]{:S(2)}, u32[]{:S(2)}) %collective-permute-start.1) | collective-permute-done | bytes 983072 | tf_op jit(solution)/shard_map/ppermute | solution.py:304
  178.9 1.9 select_select_fusion
  180.9 1.4 broadcast_select_fusion.1
  183.0 1.1 copy.37
  186.3 1.2 copy.38
  191.7 25.2 %all-to-all-done = bf16[1,128,2,4,768]{4,1,2,0,3:T(8,128)(2,1)} async-done(((bf16[1,128,2,4,768]{4,1,2,0,3:T(8,128)(2,1)}), bf16[1,128,2,4,768]{4,1,2,0,3:T(8,128)(2,1)}, u32[]{:S(2)}, u32[]{:S(2)}) %all-to-all-start) | async-done | bytes 1572896 | tf_op jit(solution)/shard_map/all_to_all | solution.py:362
  216.9 1.5 fusion.72
  218.4 13.8 %shard_map.201 = bf16[640,768]{1,0:T(8,128)(2,1)S(1)} custom-call(s32[1]{0:T(128)} %bitcast.10.patch_ref, s32[1]{0:T(128)S(6)} %copy.43.count_ref, bf16[640,768]{1,0:T(8,128)(2,1)S(1)} %get-tuple-element.21.q_ref, bf16[640,768]{1,0:T(8,128)(2,1)S(1)} %get-tuple-element.20.k_ref, bf16[640,768]{1,0:T(8,128)(2,1)S(1)} %get-tuple-element.16.v_ref, ...), custom_call_target="tpu_custom_call" | custom-call | flops 2013265920 | bytes 5505024 | tf_op jit(solution)/shard_map/pallas_call | solution.py:265
  232.2 1.0 slice.152
  233.2 17.7 %all_gather.26 = bf16[128,3072]{1,0:T(8,128)(2,1)S(1)} all-gather(bf16[128,768]{1,0:T(8,128)(2,1)S(1)} %slice.151), channel_id=1, replica_groups=mesh['section'=2,'grp'=4,'tok'=4] {'tok'}, dimensions={1}, use_global_device_ids=true | all-gather | bytes 983040 | tf_op jit(solution)/shard_map/all_gather | solution.py:386
  251.6 3.1 fusion.40
  254.7 24.9 %all_gather.27 = bf16[128,3072]{1,0:T(8,128)(2,1)S(1)} all-gather(bf16[128,768]{1,0:T(8,128)(2,1)S(1)} %fusion.40), channel_id=1, replica_groups=mesh['section'=2,'grp'=4,'tok'=4] {'tok'}, dimensions={1}, use_global_device_ids=true | all-gather | bytes 983040 | tf_op jit(solution)/shard_map/all_gather | solution.py:390
  279.6 1.5 fusion.71
  281.8 18.2 %fusion.13 = bf16[128,3072]{1,0:T(8,128)(2,1)} fusion(bf16[1,3072,3072]{2,1,0:T(8,128)(2,1)} %param.31, bf16[1,3072,3072]{2,1,0:T(8,128)(2,1)} %param.30, f32[128,3072]{1,0:T(8,128)S(1)} %get-tuple-element.15, f32[3072]{0:T(1024)S(1)} %bitcast.143, f32[3072]{0:T(1024)S(1)} %bitcast.144, f32[128]{0:T(128)S(1)} %add_rsqrt_fusion.3, ...), kind=kOutput, calls=%fused_computation.13 | convolution fusion | flops 4837736448 | bytes 40133632 | tf_op jit(solution)/shard_map/dot_general | solution.py:405
  300.0 5.2 %all-to-all-start.1 = ((bf16[4,32,3072]{2,1,0:T(8,128)(2,1)}), bf16[4,32,3072]{2,1,0:T(8,128)(2,1)}, u32[]{:S(2)}, u32[]{:S(2)}) async-start(bf16[4,32,3072]{2,1,0:T(8,128)(2,1)} %bitcast.32), calls=%async_computation.1 | async-start | bytes 1572864 | tf_op jit(solution)/shard_map/all_to_all | solution.py:406
  305.3 2.6 copy.39
  307.9 2.0 reshape.194
  309.9 25.8 %all-gather.9.cloned.1.call-done = bf16[2048,768]{1,0:T(8,128)(2,1)} async-done(((bf16[512,768]{1,0:T(8,128)(2,1)}), bf16[2048,768]{1,0:T(8,128)(2,1)}) %all-gather.9.cloned.1.call-update) | async-done | bytes 3145744 | tf_op jit(solution)/shard_map/all_gather | solution.py:388
  335.7 6.8 %bitcast_convert_fusion = bf16[512,768]{1,0:T(8,128)(2,1)} fusion(bf16[4,512,768]{2,1,0:T(8,128)(2,1)} %bitcast.150, bf16[4,768,768]{2,1,0:T(8,128)(2,1)} %bitcast.149), kind=kOutput, calls=%fused_computation.37 | convolution fusion | flops 2416312320 | bytes 8650752 | tf_op jit(solution)/shard_map/trd,tdc->rc/dot_general | solution.py:391
  342.5 4.3 %all-to-all-start.2 = ((bf16[4,128,768]{2,1,0:T(8,128)(2,1)}), bf16[4,128,768]{2,1,0:T(8,128)(2,1)}, u32[]{:S(2)}, u32[]{:S(2)}) async-start(bf16[4,128,768]{2,1,0:T(8,128)(2,1)} %bitcast.133), calls=%async_computation.2 | async-start | bytes 1572864 | tf_op jit(solution)/shard_map/all_to_all | solution.py:397
  346.9 1.3 broadcast_select_fusion
  348.2 1.3 convert_reduce_fusion.1
  349.5 1.5 collective-permute-start.2
  351.0 16.5 %all-to-all-done.2 = bf16[4,128,768]{2,1,0:T(8,128)(2,1)} async-done(((bf16[4,128,768]{2,1,0:T(8,128)(2,1)}), bf16[4,128,768]{2,1,0:T(8,128)(2,1)}, u32[]{:S(2)}, u32[]{:S(2)}) %all-to-all-start.2) | async-done | bytes 786464 | tf_op jit(solution)/shard_map/all_to_all | solution.py:397
  367.5 1.3 convert_bitcast_fusion.1
  369.0 1.0 copy-done.3
  370.1 1.4 collective-permute-start.3
  372.9 16.0 %collective-permute-done.3 = bf16[128,3072]{1,0:T(8,128)(2,1)S(1)} collective-permute-done((bf16[128,3072]{1,0:T(8,128)(2,1)S(1)}, bf16[128,3072]{1,0:T(8,128)(2,1)S(1)}, u32[]{:S(2)}, u32[]{:S(2)}) %collective-permute-start.3) | collective-permute-done | bytes 786464 | tf_op jit(solution)/shard_map/ppermute | solution.py:20
  (84 shorter events, 11.1 us)
Async XLA Ops:
  7.2 364.8 %copy-start = (bf16[3072,32]{0,1:T(8,128)(2,1)S(1)}, bf16[3072,32]{0,1:T(8,128)(2,1)}, u32[]{:S(2)}) copy-start(bf16[3072,32]{0,1:T(8,128)(2,1)} %param.34) | copy-start | bytes 589828
  7.2 12.1 %copy-start.2 = (bf16[1,1,128,3072]{3,2,1,0:T(8,128)(2,1)S(1)}, bf16[1,1,128,3072]{3,2,1,0:T(8,128)(2,1)}, u32[]{:S(2)}) copy-start(bf16[1,1,128,3072]{3,2,1,0:T(8,128)(2,1)} %param.19) | copy-start | bytes 2359300
  7.2 92.9 %all-gather.7.cloned.1.call-start = ((), (), s32[]{:S(2)}) async-start(), calls=%async_computation.3 | async-start | bytes 4915200 | tf_op jit(solution)/shard_map/all_gather | solution.py:360
  16.4 3.3 copy-start.9
  19.7 1.8 copy-start.4
  21.5 1.6 copy-start.12
  101.4 12.7 %slice-start = ((s8[14155776]{0:T(1024)(128)(4,1)}), s8[4194304]{0:T(1024)(128)(4,1)S(1)}, s32[]{:S(2)}) async-start(s8[14155776]{0:T(1024)(128)(4,1)} %bitcast.147), calls=%async_computation.6 | async-start | bytes 8388608
  105.2 8.9 %slice-start.1 = ((s8[14155776]{0:T(1024)(128)(4,1)}), s8[4194304]{0:T(1024)(128)(4,1)S(1)}, s32[]{:S(2)}) async-start(s8[14155776]{0:T(1024)(128)(4,1)} %bitcast.147), calls=%async_computation.7 | async-start | bytes 8388608
  106.9 7.3 %slice-start.2 = ((s8[14155776]{0:T(1024)(128)(4,1)}), s8[4194304]{0:T(1024)(128)(4,1)S(1)}, s32[]{:S(2)}) async-start(s8[14155776]{0:T(1024)(128)(4,1)} %bitcast.147), calls=%async_computation.8 | async-start | bytes 8388608
  106.9 7.3 %slice-start.3 = ((s8[14155776]{0:T(1024)(128)(4,1)}), s8[1572864]{0:T(1024)(128)(4,1)S(1)}, s32[]{:S(2)}) async-start(s8[14155776]{0:T(1024)(128)(4,1)} %bitcast.147), calls=%async_computation.9 | async-start | bytes 3145728
  114.1 7.8 %copy-start.6 = (bf16[128,2304]{1,0:T(8,128)(2,1)}, bf16[128,2304]{1,0:T(8,128)(2,1)S(1)}, u32[]{:S(2)}) copy-start(bf16[128,2304]{1,0:T(8,128)(2,1)S(1)} %fusion.16) | copy-start | bytes 1769476
  121.9 2.8 copy-start.1
  123.5 45.9 %collective-permute-start = (bf16[640,768]{1,0:T(8,128)(2,1)}, bf16[640,768]{1,0:T(8,128)(2,1)S(1)}, u32[]{:S(2)}, u32[]{:S(2)}) collective-permute-start(bf16[640,768]{1,0:T(8,128)(2,1)} %get-tuple-element.19), channel_id=1, source_target_pairs={{0,1},{1,0},{2,3},{3,2},{4,5},{5,4},{6,7},{7,6},{8,9},{9,8},{10,11... | collective-permute-start | bytes 2949128 | tf_op jit(solution)/shard_map/ppermute | solution.py:303
  123.5 55.4 %collective-permute-start.1 = (bf16[640,768]{1,0:T(8,128)(2,1)}, bf16[640,768]{1,0:T(8,128)(2,1)}, u32[]{:S(2)}, u32[]{:S(2)}) collective-permute-start(bf16[640,768]{1,0:T(8,128)(2,1)} %get-tuple-element.18), channel_id=1, source_target_pairs={{0,2},{2,0},{1,3},{3,1},{4,6},{6,4},{5,7},{7,5},{8,10},{10,8},{9,1... | collective-permute-start | bytes 2949128 | tf_op jit(solution)/shard_map/ppermute | solution.py:304
  127.9 89.0 %all-to-all-start = ((bf16[1,128,2,4,768]{4,1,2,0,3:T(8,128)(2,1)}), bf16[1,128,2,4,768]{4,1,2,0,3:T(8,128)(2,1)}, u32[]{:S(2)}, u32[]{:S(2)}) async-start(bf16[1,128,2,4,768]{4,1,2,0,3:T(8,128)(2,1)} %copy.35), calls=%async_computation | async-start | bytes 3145728 | tf_op jit(solution)/shard_map/all_to_all | solution.py:362
  132.4 172.9 %all-gather.11.cloned.1.call-start = ((), (), s32[]{:S(2)}) async-start(), calls=%async_computation.5 | async-start | bytes 1966080 | tf_op jit(solution)/shard_map/all_gather | solution.py:376
  169.4 0.9 copy-start.7
  178.9 1.9 copy-start.8
  189.0 146.7 %all-gather.9.cloned.1.call-start = ((), (), s32[]{:S(2)}) async-start(), calls=%async_computation.4 | async-start | bytes 3932160 | tf_op jit(solution)/shard_map/all_gather | solution.py:388
  232.2 18.8 %copy-start.15 = (bf16[4,6144]{1,0:T(4,128)(2,1)S(1)}, bf16[4,6144]{1,0:T(4,128)(2,1)}, u32[]{:S(2)}) copy-start(bf16[4,6144]{1,0:T(4,128)(2,1)} %param.33) | copy-start | bytes 147460
  251.6 28.0 %copy-start.11 = (f32[1,1,3072]{2,1,0:T(1,128)S(1)}, f32[1,1,3072]{2,1,0:T(1,128)}, u32[]{:S(2)}) copy-start(f32[1,1,3072]{2,1,0:T(1,128)} %get-tuple-element.29) | copy-start | bytes 36868
  281.1 0.7 copy-start.13
  281.1 0.7 copy-start.14
  300.0 42.5 %all-to-all-start.1 = ((bf16[4,32,3072]{2,1,0:T(8,128)(2,1)}), bf16[4,32,3072]{2,1,0:T(8,128)(2,1)}, u32[]{:S(2)}, u32[]{:S(2)}) async-start(bf16[4,32,3072]{2,1,0:T(8,128)(2,1)} %bitcast.32), calls=%async_computation.1 | async-start | bytes 1572864 | tf_op jit(solution)/shard_map/all_to_all | solution.py:406
  342.5 4.3 %copy-start.5 = (bf16[1,1,128,6144]{3,2,1,0:T(8,128)(2,1)S(1)}, bf16[1,1,128,6144]{3,2,1,0:T(8,128)(2,1)}, u32[]{:S(2)}) copy-start(bf16[1,1,128,6144]{3,2,1,0:T(8,128)(2,1)} %param.32) | copy-start | bytes 4718596
  342.5 25.0 %all-to-all-start.2 = ((bf16[4,128,768]{2,1,0:T(8,128)(2,1)}), bf16[4,128,768]{2,1,0:T(8,128)(2,1)}, u32[]{:S(2)}, u32[]{:S(2)}) async-start(bf16[4,128,768]{2,1,0:T(8,128)(2,1)} %bitcast.133), calls=%async_computation.2 | async-start | bytes 1572864 | tf_op jit(solution)/shard_map/all_to_all | solution.py:397
  346.9 2.6 copy-start.10
  349.5 22.0 %collective-permute-start.2 = (bf16[32,3072]{1,0:T(8,128)(2,1)S(1)}, bf16[32,3072]{1,0:T(8,128)(2,1)S(1)}, u32[]{:S(2)}, u32[]{:S(2)}) collective-permute-start(bf16[32,3072]{1,0:T(8,128)(2,1)S(1)} %add_convert_fusion.5), channel_id=1, source_target_pairs={{16,0},{0,16},{17,1},{1,17},{18,2},{2,18},{19,3},{3,19},{20,4},{4,... | collective-permute-start | bytes 589832 | tf_op jit(solution)/shard_map/ppermute | solution.py:20
  368.8 1.1 copy-start.3
  369.9 2.1 copy-start.16
  370.1 18.7 %collective-permute-start.3 = (bf16[128,3072]{1,0:T(8,128)(2,1)S(1)}, bf16[128,3072]{1,0:T(8,128)(2,1)S(1)}, u32[]{:S(2)}, u32[]{:S(2)}) collective-permute-start(bf16[128,3072]{1,0:T(8,128)(2,1)S(1)} %fusion.27), channel_id=1, source_target_pairs={{16,0},{0,16},{17,1},{1,17},{18,2},{2,18},{19,3},{3,19},{20,4},{4,... | collective-permute-start | bytes 2359304 | tf_op jit(solution)/shard_map/ppermute | solution.py:20
Sparse Core Ops, SparseCore 0:
  20.9 79.1 all-gather.6
  189.1 39.6 all-gather.10
  251.1 84.5 all-gather.8

commit v3 on v2

--- a/solution.py
+++ b/solution.py
@@ -355,15 +355,14 @@
     )
     stale = stale_cache[0, 0]
     cache_rows = stale.shape[0]
+    stale_heads = lax.all_to_all(
+        stale.reshape(cache_rows, 2, count, share), "tok", split_axis=2, concat_axis=0, tiled=False
+    )
+    stale_k = stale_heads[:, :, 0].reshape(count * cache_rows, share)
+    stale_v = stale_heads[:, :, 1].reshape(count * cache_rows, share)
     text_normed = modulate(text_x, text_mod[0], text_mod[1]).astype(bf16)
     own = jnp.concatenate([image_in[0, 0], text_normed], axis=0)
     every = lax.all_gather(own, "tok", axis=0, tiled=False)
-    every, late_stale = lax.optimization_barrier((every, stale))
-    stale_heads = lax.all_to_all(
-        late_stale.reshape(cache_rows, 2, count, share), "tok", split_axis=2, concat_axis=0, tiled=False
-    )
-    stale_k = stale_heads[:, :, 0].reshape(count * cache_rows, share)
-    stale_v = stale_heads[:, :, 1].reshape(count * cache_rows, share)
     every_image_x = every[:, :image_rows].reshape(patch_len, width).astype(f32)
     every_text = every[:, image_rows:].reshape(count * text_rows, width)
     every_image = modulate(every_image_x, modul[0], modul[1]).astype(bf16)

time: 398 us -> 414 us (1.040)
  waiting for transfers between devices: 205 us -> 220 us
    all_gather x1, waiting for transfers between devices: 0.02 us -> 38.3 us  [shards_by_head(): lax.all_gather(jnp.stack([image_key, value[:patch_len]], axis=0), 'tok',...]
    all_gather x1, waiting for transfers between devices: 25.8 us -> 0.01 us  [shards_by_head(): text_att = lax.all_gather(text_own, 'tok', axis=0, tiled=False)]
    all_to_all x1, waiting for transfers between devices: 0.01 us -> 25.3 us  [shards_by_head(): lax.all_to_all(partial.astype(bf16).reshape(count, image_rows, width), 't...]
    all_to_all x1, waiting for transfers between devices: 25.2 us -> 0.01 us  [shards_by_head(): lax.all_to_all(stale.reshape(cache_rows, 2, count, share), 'tok', split_a...]
    all_gather x1, waiting for transfers between devices: 76.3 us -> 99.8 us  [shards_by_head(): every = lax.all_gather(own, 'tok', axis=0, tiled=False)]
    all_to_all x1, waiting for transfers between devices: 16.5 us -> 0.01 us  [shards_by_head(): lax.all_to_all(text_back_cols, 'tok', split_axis=0, concat_axis=1, tiled=...]
    ppermute x1, waiting for transfers between devices: 8.54 us -> 2.11 us  [swap_heads(): lax.ppermute(jnp.where(even, third, first), 'tok', [(0, 2), (2, 0), (1, 3...]
    dot_general x1, matrix products: 7.2 us -> 2.09 us  [shards_by_head(): jnp.dot(every_image, image_to_heads[0], preferred_element_type=f32)]
  transfers between devices with their start and end apart: 10 -> 10, of which waited for: 7 -> 6; matrix products, arithmetic and copies ran while one was open for 15% -> 18% of each run, Pallas kernels for 3% -> 0%
where the time goes in v3:
time: 414 us; the launch traced here: 413 us
  waiting for transfers between devices  220 us (53%)
  matrix products  43.5 us (11%)
  blocking collectives  42.5 us (10%)
  other arithmetic  24.4 us (6%)
  local copies, waits for them, and re-layouts  24.1 us (6%)
  between operations  23.4 us (6%)
  starting transfers between devices  20.9 us (5%)
  Pallas kernels  14 us (3%)
    all_gather x1, waiting for transfers between devices, shards_by_head(): every = lax.all_gather(own, 'tok', axis=0, tiled=False)  99.8 us
    all_gather x1, waiting for transfers between devices, shards_by_head(): lax.all_gather(jnp.stack([image_key, value[:patch_len]], axis=0), 'tok',...  38.3 us
    ppermute x1, waiting for transfers between devices, swap_heads(): near = lax.ppermute(second, 'tok', [(0, 1), (1, 0), (2, 3), (3, 2)])  38.1 us
    all_to_all x1, waiting for transfers between devices, shards_by_head(): lax.all_to_all(partial.astype(bf16).reshape(count, image_rows, width), 't...  25.3 us
    all_gather x1, blocking collectives, shards_by_head(): image_back = lax.all_gather(image_back_cols, 'tok', axis=1, tiled=True)  24 us
    dot_general x1, matrix products, shards_by_head(): partial = jnp.dot(hidden, image_down[0], preferred_element_type=f32)  18.7 us
    all_gather x1, blocking collectives, shards_by_head(): image_att = lax.all_gather(attended[:patch_len], 'tok', axis=1, tiled=True)  18.5 us
    ppermute x2, waiting for transfers between devices, from_behind(): return lax.ppermute(block, axis, route)  16.4 us
  transfers between devices with their start and end apart: 10, of which 6 were waited for; matrix products, arithmetic and copies ran while one was open for 18% of the time, Pallas kernels for 0%

profile of v3, /device:TPU:0, one launch (start us, length us, event | category | flops | bytes accessed | tf_op | source)
XLA Modules:
  0.0 413.0 jit_solution(6879997327671836912)
XLA Ops:
  7.2 1.4 fusion.75
  12.6 1.3 constant_dynamic-slice_fusion
  15.9 0.9 dynamic-slice_convert_fusion.1
  16.9 1.4 convert_reduce_fusion
  18.2 1.5 fusion.23
  20.2 1.0 pad_maximum_fusion.1
  21.9 1.6 copy.34
  23.5 2.6 copy.35
  26.0 6.4 %all-to-all-start = ((bf16[1,128,2,4,768]{4,1,2,0,3:T(8,128)(2,1)}), bf16[1,128,2,4,768]{4,1,2,0,3:T(8,128)(2,1)S(1)}, u32[]{:S(2)}, u32[]{:S(2)}) async-start(bf16[1,128,2,4,768]{4,1,2,0,3:T(8,128)(2,1)} %copy.35), calls=%async_computation | async-start | bytes 3145728 | tf_op jit(solution)/shard_map/all_to_all | solution.py:358
  33.2 99.8 %all-gather.7.cloned.1.call-done = bf16[640,3072]{1,0:T(8,128)(2,1)} async-done(((bf16[160,3072]{1,0:T(8,128)(2,1)}), bf16[640,3072]{1,0:T(8,128)(2,1)}) %all-gather.7.cloned.1.call-update) | async-done | bytes 3932176 | tf_op jit(solution)/shard_map/all_gather | solution.py:365
  133.0 1.3 convert_reduce_fusion.2
  134.4 2.1 slice.146
  136.5 1.5 multiply_reduce_fusion.1
  138.0 11.7 %fusion.10 = bf16[512,2304]{1,0:T(8,128)(2,1)S(1)} fusion(bf16[512,3072]{1,0:T(8,128)(2,1)S(1)} %bitcast.130, bf16[1,3072,2304]{2,1,0:T(8,128)(2,1)} %param.26), kind=kOutput, calls=%fused_computation.10 | convolution fusion | flops 7248936960 | bytes 19660800 | tf_op jit(solution)/shard_map/dot_general | solution.py:370
  149.8 2.1 add_convert_fusion.1
  151.9 2.1 fusion.16
  154.1 1.5 broadcast_select_fusion.2
  155.6 1.9 collective-permute-start.1
  161.4 38.1 %collective-permute-done = bf16[640,768]{1,0:T(8,128)(2,1)} collective-permute-done((bf16[640,768]{1,0:T(8,128)(2,1)}, bf16[640,768]{1,0:T(8,128)(2,1)}, u32[]{:S(2)}, u32[]{:S(2)}) %collective-permute-start) | collective-permute-done | bytes 983072 | tf_op jit(solution)/shard_map/ppermute | solution.py:303
  199.5 2.1 collective-permute-done.1
  201.6 1.8 select_select_fusion
  203.4 1.7 broadcast_select_fusion.1
  205.1 14.0 %shard_map.201 = bf16[640,768]{1,0:T(8,128)(2,1)S(1)} custom-call(s32[1]{0:T(128)} %bitcast.9.patch_ref, s32[1]{0:T(128)S(6)} %copy.43.count_ref, bf16[640,768]{1,0:T(8,128)(2,1)S(1)} %get-tuple-element.17.q_ref, bf16[640,768]{1,0:T(8,128)(2,1)S(1)} %get-tuple-element.16.k_ref, bf16[640,768]{1,0:T(8,128)(2,1)S(1)} %get-tuple-element.12.v_ref, ...), custom_call_target="tpu_custom_call" | custom-call | flops 2013265920 | bytes 5505024 | tf_op jit(solution)/shard_map/pallas_call | solution.py:265
  219.1 0.9 slice.154
  220.0 18.5 %all_gather.26 = bf16[128,3072]{1,0:T(8,128)(2,1)} all-gather(bf16[128,768]{1,0:T(8,128)(2,1)S(1)} %slice.153), channel_id=1, replica_groups=mesh['section'=2,'grp'=4,'tok'=4] {'tok'}, dimensions={1}, use_global_device_ids=true | all-gather | bytes 983040 | tf_op jit(solution)/shard_map/all_gather | solution.py:385
  238.6 3.4 fusion.40
  242.0 24.0 %all_gather.27 = bf16[128,3072]{1,0:T(8,128)(2,1)S(1)} all-gather(bf16[128,768]{1,0:T(8,128)(2,1)S(1)} %fusion.40), channel_id=1, replica_groups=mesh['section'=2,'grp'=4,'tok'=4] {'tok'}, dimensions={1}, use_global_device_ids=true | all-gather | bytes 983040 | tf_op jit(solution)/shard_map/all_gather | solution.py:389
  266.0 1.5 fusion.71
  267.5 1.1 copy-done.5
  269.0 18.7 %fusion.13 = bf16[128,3072]{1,0:T(8,128)(2,1)} fusion(bf16[1,3072,3072]{2,1,0:T(8,128)(2,1)} %param.31, bf16[1,3072,3072]{2,1,0:T(8,128)(2,1)} %param.30, f32[128,3072]{1,0:T(8,128)} %copy-done.5, f32[3072]{0:T(1024)S(1)} %bitcast.145, f32[3072]{0:T(1024)S(1)} %bitcast.146, f32[128]{0:T(128)S(1)} %add_rsqrt_fusion.3, f32[128]{0:T(128)S(1)} %broadcast_multiply_fusion.2), kind=kOutput, calls=%fused_computation.13 | convolution fusion | flops 4837736448 | bytes 40133632 | tf_op jit(solution)/shard_map/dot_general | solution.py:404
  287.6 5.5 %all-to-all-start.1 = ((bf16[4,32,3072]{2,1,0:T(8,128)(2,1)}), bf16[4,32,3072]{2,1,0:T(8,128)(2,1)}, u32[]{:S(2)}, u32[]{:S(2)}) async-start(bf16[4,32,3072]{2,1,0:T(8,128)(2,1)} %bitcast.134), calls=%async_computation.1 | async-start | bytes 1572864 | tf_op jit(solution)/shard_map/all_to_all | solution.py:405
  293.9 1.2 copy.37
  295.9 1.2 copy.38
  297.2 0.8 pad_maximum_fusion.2
  298.0 25.3 %all-to-all-done.1 = bf16[4,32,3072]{2,1,0:T(8,128)(2,1)} async-done(((bf16[4,32,3072]{2,1,0:T(8,128)(2,1)}), bf16[4,32,3072]{2,1,0:T(8,128)(2,1)}, u32[]{:S(2)}, u32[]{:S(2)}) %all-to-all-start.1) | async-done | bytes 786464 | tf_op jit(solution)/shard_map/all_to_all | solution.py:405
  323.3 1.3 convert_reduce_fusion.1
  324.6 1.0 add_convert_fusion.5
  325.7 1.6 collective-permute-start.2
  327.3 6.8 %bitcast_convert_fusion = bf16[512,768]{1,0:T(8,128)(2,1)} fusion(bf16[4,512,768]{2,1,0:T(8,128)(2,1)} %bitcast.150, bf16[4,768,768]{2,1,0:T(8,128)(2,1)} %bitcast.149), kind=kOutput, calls=%fused_computation.37 | convolution fusion | flops 2416312320 | bytes 8650752 | tf_op jit(solution)/shard_map/trd,tdc->rc/dot_general | solution.py:390
  334.1 3.8 all-to-all-start.2
  339.1 0.9 fusion.44
  340.0 38.3 %all-gather.11.cloned.1.call-done = bf16[8,128,768]{2,1,0:T(8,128)(2,1)} async-done(((bf16[2,128,768]{2,1,0:T(8,128)(2,1)}), bf16[8,128,768]{2,1,0:T(8,128)(2,1)}) %all-gather.11.cloned.1.call-update) | async-done | bytes 1572880 | tf_op jit(solution)/shard_map/all_gather | solution.py:375
  378.2 3.8 copy.39
  382.0 3.0 reshape.194
  385.6 1.5 collective-permute-start.3
  387.1 1.3 broadcast_select_fusion
  388.5 16.4 %collective-permute-done.3 = bf16[128,3072]{1,0:T(8,128)(2,1)S(1)} collective-permute-done((bf16[128,3072]{1,0:T(8,128)(2,1)S(1)}, bf16[128,3072]{1,0:T(8,128)(2,1)S(1)}, u32[]{:S(2)}, u32[]{:S(2)}) %collective-permute-start.3) | collective-permute-done | bytes 786464 | tf_op jit(solution)/shard_map/ppermute | solution.py:20
  405.6 0.9 copy.45
  (86 shorter events, 6.9 us)
Async XLA Ops:
  7.2 331.9 %copy-start = (bf16[3072,32]{0,1:T(8,128)(2,1)S(1)}, bf16[3072,32]{0,1:T(8,128)(2,1)}, u32[]{:S(2)}) copy-start(bf16[3072,32]{0,1:T(8,128)(2,1)} %param.34) | copy-start | bytes 589828
  7.2 12.6 %copy-start.2 = (bf16[1,1,128,3072]{3,2,1,0:T(8,128)(2,1)S(1)}, bf16[1,1,128,3072]{3,2,1,0:T(8,128)(2,1)}, u32[]{:S(2)}) copy-start(bf16[1,1,128,3072]{3,2,1,0:T(8,128)(2,1)} %param.19) | copy-start | bytes 2359300
  7.2 125.8 %all-gather.7.cloned.1.call-start = ((), (), s32[]{:S(2)}) async-start(), calls=%async_computation.3 | async-start | bytes 4915200 | tf_op jit(solution)/shard_map/all_gather | solution.py:365
  16.9 3.3 copy-start.8
  20.1 1.8 copy-start.6
  26.0 6.5 %copy-start.12 = (bf16[1,4,18432]{2,1,0:T(4,128)(2,1)S(1)}, bf16[1,4,18432]{2,1,0:T(4,128)(2,1)}, u32[]{:S(2)}) copy-start(bf16[1,4,18432]{2,1,0:T(4,128)(2,1)} %param.23) | copy-start | bytes 442372
  26.0 135.3 %all-to-all-start = ((bf16[1,128,2,4,768]{4,1,2,0,3:T(8,128)(2,1)}), bf16[1,128,2,4,768]{4,1,2,0,3:T(8,128)(2,1)S(1)}, u32[]{:S(2)}, u32[]{:S(2)}) async-start(bf16[1,128,2,4,768]{4,1,2,0,3:T(8,128)(2,1)} %copy.35), calls=%async_computation | async-start | bytes 3145728 | tf_op jit(solution)/shard_map/all_to_all | solution.py:358
  32.5 294.8 %all-gather.9.cloned.1.call-start = ((), (), s32[]{:S(2)}) async-start(), calls=%async_computation.4 | async-start | bytes 3932160 | tf_op jit(solution)/shard_map/all_gather | solution.py:387
  138.0 13.9 %slice-start = ((s8[14155776]{0:T(1024)(128)(4,1)}), s8[4194304]{0:T(1024)(128)(4,1)S(1)}, s32[]{:S(2)}) async-start(s8[14155776]{0:T(1024)(128)(4,1)} %bitcast.119), calls=%async_computation.6 | async-start | bytes 8388608
  138.0 13.9 %slice-start.1 = ((s8[14155776]{0:T(1024)(128)(4,1)}), s8[4194304]{0:T(1024)(128)(4,1)S(1)}, s32[]{:S(2)}) async-start(s8[14155776]{0:T(1024)(128)(4,1)} %bitcast.119), calls=%async_computation.7 | async-start | bytes 8388608
  138.0 13.9 %slice-start.2 = ((s8[14155776]{0:T(1024)(128)(4,1)}), s8[4194304]{0:T(1024)(128)(4,1)S(1)}, s32[]{:S(2)}) async-start(s8[14155776]{0:T(1024)(128)(4,1)} %bitcast.119), calls=%async_computation.8 | async-start | bytes 8388608
  138.0 13.9 %slice-start.3 = ((s8[14155776]{0:T(1024)(128)(4,1)}), s8[1572864]{0:T(1024)(128)(4,1)S(1)}, s32[]{:S(2)}) async-start(s8[14155776]{0:T(1024)(128)(4,1)} %bitcast.119), calls=%async_computation.9 | async-start | bytes 3145728
  149.8 4.3 %copy-start.3 = (bf16[512,2304]{1,0:T(8,128)(2,1)}, bf16[512,2304]{1,0:T(8,128)(2,1)S(1)}, u32[]{:S(2)}) copy-start(bf16[512,2304]{1,0:T(8,128)(2,1)S(1)} %fusion.10) | copy-start | bytes 7077892
  154.0 3.5 copy-start.1
  154.1 6.6 %copy-start.15 = (bf16[4,6144]{1,0:T(4,128)(2,1)S(1)}, bf16[4,6144]{1,0:T(4,128)(2,1)}, u32[]{:S(2)}) copy-start(bf16[4,6144]{1,0:T(4,128)(2,1)} %param.33) | copy-start | bytes 147460
  155.6 43.9 %collective-permute-start = (bf16[640,768]{1,0:T(8,128)(2,1)}, bf16[640,768]{1,0:T(8,128)(2,1)}, u32[]{:S(2)}, u32[]{:S(2)}) collective-permute-start(bf16[640,768]{1,0:T(8,128)(2,1)} %get-tuple-element.15), channel_id=1, source_target_pairs={{0,1},{1,0},{2,3},{3,2},{4,5},{5,4},{6,7},{7,6},{8,9},{9,8},{10,11... | collective-permute-start | bytes 2949128 | tf_op jit(solution)/shard_map/ppermute | solution.py:303
  155.6 46.0 %collective-permute-start.1 = (bf16[640,768]{1,0:T(8,128)(2,1)}, bf16[640,768]{1,0:T(8,128)(2,1)}, u32[]{:S(2)}, u32[]{:S(2)}) collective-permute-start(bf16[640,768]{1,0:T(8,128)(2,1)} %get-tuple-element.14), channel_id=1, source_target_pairs={{0,2},{2,0},{1,3},{3,1},{4,6},{6,4},{5,7},{7,5},{8,10},{10,8},{9,1... | collective-permute-start | bytes 2949128 | tf_op jit(solution)/shard_map/ppermute | solution.py:304
  161.3 40.3 %copy-start.4 = (bf16[512,2304]{1,0:T(8,128)(2,1)S(1)}, bf16[512,2304]{1,0:T(8,128)(2,1)}, u32[]{:S(2)}) copy-start(bf16[512,2304]{1,0:T(8,128)(2,1)} %copy-done.3) | copy-start | bytes 7077892
  238.6 27.4 %copy-start.11 = (f32[1,1,3072]{2,1,0:T(1,128)S(1)}, f32[1,1,3072]{2,1,0:T(1,128)}, u32[]{:S(2)}) copy-start(f32[1,1,3072]{2,1,0:T(1,128)} %get-tuple-element.25) | copy-start | bytes 36868
  267.5 1.2 copy-start.5
  267.5 1.5 copy-start.13
  267.5 1.5 copy-start.14
  287.6 5.5 %copy-start.16 = (f32[128]{0:T(128)S(1)}, f32[128]{0:T(128)}, u32[]{:S(2)}) copy-start(f32[128]{0:T(128)} %slice_bitcast_fusion.1) | copy-start | bytes 1540
  287.6 35.7 %all-to-all-start.1 = ((bf16[4,32,3072]{2,1,0:T(8,128)(2,1)}), bf16[4,32,3072]{2,1,0:T(8,128)(2,1)}, u32[]{:S(2)}, u32[]{:S(2)}) async-start(bf16[4,32,3072]{2,1,0:T(8,128)(2,1)} %bitcast.134), calls=%async_computation.1 | async-start | bytes 1572864 | tf_op jit(solution)/shard_map/all_to_all | solution.py:405
  293.1 85.1 %all-gather.11.cloned.1.call-start = ((), (), s32[]{:S(2)}) async-start(), calls=%async_computation.5 | async-start | bytes 1966080 | tf_op jit(solution)/shard_map/all_gather | solution.py:375
  297.1 27.5 %copy-start.10 = (f32[1,1,3072]{2,1,0:T(1,128)S(1)}, f32[1,1,3072]{2,1,0:T(1,128)}, u32[]{:S(2)}) copy-start(f32[1,1,3072]{2,1,0:T(1,128)} %get-tuple-element.20) | copy-start | bytes 36868
  325.7 13.0 %collective-permute-start.2 = (bf16[32,3072]{1,0:T(8,128)(2,1)S(1)}, bf16[32,3072]{1,0:T(8,128)(2,1)S(1)}, u32[]{:S(2)}, u32[]{:S(2)}) collective-permute-start(bf16[32,3072]{1,0:T(8,128)(2,1)S(1)} %add_convert_fusion.5), channel_id=1, source_target_pairs={{16,0},{0,16},{17,1},{1,17},{18,2},{2,18},{19,3},{3,19},{20,4},{4,... | collective-permute-start | bytes 589832 | tf_op jit(solution)/shard_map/ppermute | solution.py:20
  334.1 3.9 copy-start.9
  334.1 5.0 %copy-start.17 = (f32[1,32,32]{2,1,0:T(8,128)S(1)}, f32[1,32,32]{2,1,0:T(8,128)}, u32[]{:S(2)}) copy-start(f32[1,32,32]{2,1,0:T(8,128)} %param.35) | copy-start | bytes 12292
  334.1 51.0 %all-to-all-start.2 = ((bf16[4,128,768]{2,1,0:T(8,128)(2,1)}), bf16[4,128,768]{2,1,0:T(8,128)(2,1)S(1)}, u32[]{:S(2)}, u32[]{:S(2)}) async-start(bf16[4,128,768]{2,1,0:T(8,128)(2,1)} %bitcast.37), calls=%async_computation.2 | async-start | bytes 1572864 | tf_op jit(solution)/shard_map/all_to_all | solution.py:396
  385.3 1.8 copy-start.7
  385.6 19.3 %collective-permute-start.3 = (bf16[128,3072]{1,0:T(8,128)(2,1)S(1)}, bf16[128,3072]{1,0:T(8,128)(2,1)S(1)}, u32[]{:S(2)}, u32[]{:S(2)}) collective-permute-start(bf16[128,3072]{1,0:T(8,128)(2,1)S(1)} %fusion.27), channel_id=1, source_target_pairs={{16,0},{0,16},{17,1},{1,17},{18,2},{2,18},{19,3},{3,19},{20,4},{4,... | collective-permute-start | bytes 2359304 | tf_op jit(solution)/shard_map/ppermute | solution.py:20
Sparse Core Ops, SparseCore 0:
  21.3 111.6 all-gather.6
  238.7 83.8 all-gather.8
  324.2 54.0 all-gather.10
